TPU v7x, 32 devices: a whole 2x2x4 slice. The times are simulated.
32 devices in a mesh: leaf: 8 (over y, x, core), node: 4 (over z).
Axes of the slice: x: 2, y: 2, z: 4, core: 2. Of those that a mesh axis runs over, the one named last changes fastest.
Arguments:
- positions: float32 [3, 32768], P(None, ('leaf', 'node')), may hold values from 0 to 16, as said below
- charges: float32 [32768], P(('leaf', 'node')), may hold values from -0.625 to 0.625
- near_list: int32 [64, 11], P(('leaf', 'node')), may hold values from 0 to 63, as said below
- near_count: int32 [64], P(('leaf', 'node')), may hold values from 1 to 11, as said below
- far_sample: float32 [32768, 128], P(('leaf', 'node')), may hold values from -0.625 to 0.625
- proxies: float32 [64, 3, 128], P(('leaf', 'node')), may hold values from -2 to 18, as said below
- strengths: float32 [64, 128], P(('leaf', 'node')), may hold values from 0.005 to 0.05
Outputs:
- near_potential: float32 [32768], P(('leaf', 'node'))
- leaf_coeffs: float32 [64, 128], P(('leaf', 'node'))
- top_factor: float32 [8, 128, 128], P('leaf', 'node')
- top_coeffs: float32 [8, 128], P('leaf', 'node')
Inputs may be any that keep to these rules, and one draw needn't show every extreme that they name: `near_list`: each entry of row g is a leaf other than g whose cube touches the cube of leaf g (shares a face, an edge or a corner); the entries before near_count[g] are distinct. `near_count`: slots of a row at or past its count are not used; some leaf uses all 11 slots. `positions`: the particles of leaf g lie in the unit cube whose lowest corner is (g // 4, (g // 2) % 2, g % 2). `proxies`: the proxy points of leaf g lie at distance 1.5 to 2 from the centre of its cube.
All inputs are finite; a program needn't handle non-finite values.
Results may differ from a plain program's by a relative error of at most 0.0003.
Values sent between devices are 32-bit elements; how exact they have to be, the bound alone decides.
No kernel may reach another device: no remote copies, remote signals or barrier semaphores. Data moves between devices by JAX's collectives and lax.ppermute only.
A program may use at most 64 MiB of HBM per device.

v0:
```python
import functools

import jax
import jax.numpy as jnp
from jax import lax
from jax.experimental import pallas as pl
from jax.experimental.pallas import tpu as pltpu
from jax.sharding import PartitionSpec as P

soft_square = 0.0025
HIGHEST = lax.Precision.HIGHEST
SUBLANES = 8
VMEM_SPEC = pl.BlockSpec(memory_space=pltpu.VMEM)
HBM_SPEC = pl.BlockSpec(memory_space=pltpu.HBM)
LANES = 128
COORDS = 4
VMEM_LIMIT = 24 << 20
PART_PAIRS = ((0, 0), (0, 1), (1, 0), (1, 1), (0, 2), (2, 0), (1, 2), (2, 1))


def split_parts(block):
    first = block.astype(jnp.bfloat16).astype(jnp.float32)
    rest = block - first
    second = rest.astype(jnp.bfloat16).astype(jnp.float32)
    return (first, second, rest - second)


def row_of(shape):
    return lax.broadcasted_iota(jnp.int32, shape, 0)


def square_sum_of(shifted):
    row = row_of(shifted.shape)
    return jnp.sum(jnp.where(row < 3, shifted * shifted, 0.0), axis=0, keepdims=True)


def target_factor(shifted):
    row = row_of(shifted.shape)
    norm = square_sum_of(shifted) + soft_square
    rows = jnp.where(
        row < 3, shifted, jnp.where(row == 3, norm, jnp.where(row == 4, 1.0, 0.0))
    )
    parts = split_parts(rows)
    return jnp.concatenate([parts[a] for a, _ in PART_PAIRS], axis=0)


def source_factor(shifted):
    row = row_of(shifted.shape)
    norm = square_sum_of(shifted)
    rows = jnp.where(
        row < 3, -2.0 * shifted, jnp.where(row == 3, 1.0, jnp.where(row == 4, norm, 0.0))
    )
    parts = split_parts(rows)
    return jnp.concatenate([parts[b] for _, b in PART_PAIRS], axis=0).astype(jnp.bfloat16)


def squares(target, source):
    return jnp.dot(target, source, preferred_element_type=jnp.float32)


def padded_rows(block):
    filler = jnp.zeros((SUBLANES - block.shape[0], block.shape[1]), jnp.float32)
    return jnp.concatenate([block, filler], axis=0)


def fold_rows(rank):
    return rank // 2 + SUBLANES


def fold(gram, moment):
    rank = gram.shape[1]
    half = rank // 2
    lane = lax.broadcasted_iota(jnp.int32, (half, rank), 1)
    row = row_of((half, rank))
    upper = pltpu.roll(gram[:half, :], half, 1)
    lower = gram[half:, :]
    folded = jnp.where((lane < half) | (lane - half >= row), lower, upper)
    diagonal = jnp.sum(jnp.where(lane - half == row, upper, 0.0), axis=0, keepdims=True)
    filler = jnp.zeros((SUBLANES - 2, rank), jnp.float32)
    return jnp.concatenate([folded, diagonal, moment, filler], axis=0)


def unfold(folded):
    rank = folded.shape[1]
    half = rank // 2
    lane = lax.broadcasted_iota(jnp.int32, (half, rank), 1)
    row = row_of((half, rank))
    lower = folded[:half, :]
    turned = jnp.transpose(jnp.concatenate([lower, lower], axis=0))
    mixed = pltpu.roll(lower, half, 1)
    diagonal = pltpu.roll(jnp.broadcast_to(folded[half : half + 1, :], (SUBLANES, rank)), half, 1)
    corner = jnp.where(
        row > lane, mixed, jnp.where(row < lane, turned[half:, :], diagonal[0:1, :])
    )
    top = jnp.where(lane < half, corner, turned[:half, :])
    bottom = jnp.where((lane < half) | (lane - half >= row), lower, turned[half:, :])
    return jnp.concatenate([top, bottom], axis=0), folded[half + 1 : half + 2, :]


def gram_body(
    positions_hbm,
    charges_hbm,
    far_hbm,
    proxies_hbm,
    strengths_hbm,
    payload_ref,
    target_ref,
    centre_ref,
    gram_ref,
    moment_ref,
    positions_ref,
    charges_ref,
    far_ref,
    proxies_ref,
    strengths_ref,
    sems,
):
    per_device, rank = strengths_ref.shape
    leaf_size = far_ref.shape[0] // per_device
    pieces = leaf_size // LANES
    pairs = [
        (positions_hbm, positions_ref),
        (charges_hbm, charges_ref),
        (proxies_hbm, proxies_ref),
        (strengths_hbm, strengths_ref),
    ]
    for member in range(per_device):
        span = slice(member * leaf_size, (member + 1) * leaf_size)
        pairs.append((far_hbm.at[span], far_ref.at[span]))
    copies = [
        pltpu.make_async_copy(source, target, sems.at[at])
        for at, (source, target) in enumerate(pairs)
    ]
    for copy in copies:
        copy.start()
    for copy in copies[:4]:
        copy.wait()

    points = padded_rows(positions_ref[...])
    centre = jnp.zeros((SUBLANES, 1), jnp.float32)
    for member in range(per_device):
        centre = centre + (jnp.floor(points[:, member * leaf_size : member * leaf_size + 1]) + 0.5)
    centre = jnp.where(row_of(centre.shape) < 3, centre / per_device, 0.0)
    centre_ref[...] = jnp.broadcast_to(centre, centre_ref.shape)
    shifted = points - centre
    total_gram = jnp.zeros((rank, rank), jnp.float32)
    total_moment = jnp.zeros((1, rank), jnp.float32)
    for member in range(per_device):
        span = slice(member * leaf_size, (member + 1) * leaf_size)
        for piece in range(pieces):
            at = (member * pieces + piece) * COORDS
            lanes = slice(span.start + piece * LANES, span.start + (piece + 1) * LANES)
            payload_ref[at : at + 3, :] = positions_ref[:, lanes]
            payload_ref[at + 3 : at + 4, :] = charges_ref[at // COORDS : at // COORDS + 1, :]
        target = jnp.transpose(target_factor(shifted[:, span])).astype(jnp.bfloat16)
        target_ref[span, :] = target
        proxies = jnp.concatenate([proxies_ref[c, member : member + 1, :] for c in range(3)], axis=0)
        source = source_factor(padded_rows(proxies) - centre)
        kernel_values = lax.rsqrt(squares(target, source))
        copies[4 + member].wait()
        response = far_ref[span, :] + kernel_values * strengths_ref[member : member + 1, :]
        weights = jnp.concatenate(
            [charges_ref[member * pieces + p : member * pieces + p + 1, :] for p in range(pieces)],
            axis=1,
        )
        left = jnp.concatenate(
            [jnp.transpose(response), jnp.broadcast_to(weights, (SUBLANES, leaf_size))], axis=0
        )
        both = jnp.dot(left, response, precision=HIGHEST, preferred_element_type=jnp.float32)
        gram_ref[member] = both[:rank, :]
        moment_ref[member : member + 1, :] = both[rank : rank + 1, :]
        total_gram = total_gram + both[:rank, :]
        total_moment = total_moment + both[rank : rank + 1, :]
    points_rows = per_device * pieces * COORDS
    payload_ref[points_rows:, :] = fold(total_gram, total_moment)


def lane_sums(block):
    parts = jnp.concatenate([part.astype(jnp.bfloat16) for part in split_parts(block)], axis=1)
    ones = jnp.ones((2 * SUBLANES, parts.shape[1]), jnp.bfloat16)
    sums = lax.dot_general(
        ones, parts, (((1,), (1,)), ((), ())), preferred_element_type=jnp.float32
    )
    return sums[0:1, :]


def source_blocks(source_ref, first_row, leaf_size, centre):
    blocks = [
        source_ref[pl.ds(first_row + piece * COORDS, COORDS), :]
        for piece in range(leaf_size // LANES)
    ]
    points = jnp.concatenate([padded_rows(block) - centre for block in blocks], axis=1)
    return source_factor(points), jnp.concatenate([block[3:4, :] for block in blocks], axis=1)


def add_sources(total_ref, before_ref, target_ref, items, flags, per_device, leaf_size):
    chunk = LANES
    pieces = leaf_size // LANES
    for member in range(per_device):
        weights = [
            charge * jnp.concatenate([flag[member : member + 1, :]] * pieces, axis=1)
            for (_, charge), flag in zip(items, flags)
        ]
        for start in range(member * leaf_size, (member + 1) * leaf_size, chunk):
            rows = slice(start, start + chunk)
            target = target_ref[rows, :]
            part = None if before_ref is None else before_ref[rows, :]
            for (factor, _), weight in zip(items, weights):
                term = lax.rsqrt(squares(target, factor)) * weight
                for low in range(0, leaf_size, LANES):
                    piece = term[:, low : low + LANES]
                    part = piece if part is None else part + piece
            total_ref[rows, :] = part


def own_body(
    list_hbm,
    count_hbm,
    payload_ref,
    target_ref,
    centre_ref,
    total_ref,
    flags_ref,
    list_ref,
    count_ref,
    sems,
    *,
    node_count,
):
    per_device, slots = list_ref.shape
    leaf_size = total_ref.shape[0] // per_device
    leaf_rows = leaf_size // LANES * COORDS
    half = node_count // 2
    copies = [
        pltpu.make_async_copy(list_hbm, list_ref, sems.at[0]),
        pltpu.make_async_copy(count_hbm, count_ref, sems.at[1]),
    ]
    for copy in copies:
        copy.start()
    centre = centre_ref[...]
    items = [
        source_blocks(payload_ref, leaf * leaf_rows, leaf_size, centre)
        for leaf in range(per_device)
    ]
    for copy in copies:
        copy.wait()
    node_index = lax.axis_index("node")
    block_index = lax.axis_index("leaf")
    row = row_of((per_device, slots))
    slot = lax.broadcasted_iota(jnp.int32, (per_device, slots), 1)
    used = jnp.zeros((per_device, slots), jnp.int32)
    for member in range(per_device):
        used = jnp.where(row == member, count_ref[member], used)
    listed = jnp.where(slot < used, list_ref[...], -1)
    beside = jnp.where(node_index >= half, block_index + 1, block_index - 1)
    flags = []
    for number in range(flags_ref.shape[0]):
        apart, kind, member = (
            number // (3 * per_device),
            number // per_device % 3,
            number % per_device,
        )
        device = node_index ^ (apart if kind == 0 else apart + half)
        block = beside if kind == 2 else block_index
        leaf = (block * node_count + device) * per_device + member
        hit = jnp.sum(jnp.where(listed == leaf, 1.0, 0.0), axis=1, keepdims=True)
        if number < per_device:
            hit = jnp.where(row_of(hit.shape) == number, 1.0, hit)
        flag = jnp.broadcast_to(hit, (per_device, LANES))
        flags_ref[number] = padded_rows(flag)
        if number < per_device:
            flags.append(flag)
    add_sources(total_ref, None, target_ref, items, flags, per_device, leaf_size)


def merge_body(payload_ref, other_ref, side_ref, held_ref, *, rows):
    held_ref[0:rows, :] = payload_ref[0:rows, :]
    held_ref[rows : 2 * rows, :] = other_ref[0:rows, :]
    held_ref[2 * rows : 3 * rows, :] = side_ref[0:rows, :]
    held_ref[3 * rows :, :] = payload_ref[rows:, :] + other_ref[rows:, :]


def near_body(*refs, first, last, source_count, final):
    flags_ref, centre_ref, target_ref, before_ref = refs[:4]
    source_refs = refs[4 : 4 + source_count]
    out_ref = refs[4 + source_count]
    total_ref = refs[5 + source_count] if final else out_ref
    leaf_size = LANES * COORDS
    per_device = target_ref.shape[0] // leaf_size
    leaf_rows = leaf_size // LANES * COORDS
    group = 3 * per_device
    centre = centre_ref[...]
    fresh = True

    def add_group(source_ref, row, number, skip, before_ref):
        items = [
            source_blocks(source_ref, row + leaf * leaf_rows, leaf_size, centre)
            for leaf in range(skip, group)
        ]
        flags = [flags_ref[number + leaf] for leaf in range(skip, group)]
        add_sources(total_ref, before_ref, target_ref, items, flags, per_device, leaf_size)

    number = first // group * group
    for source_ref in source_refs:
        held = (min(last - number, source_ref.shape[0] // leaf_rows)) // group
        if source_ref is not source_refs[0]:
            fresh = False
        add_group(source_ref, 0, number, first % group if fresh else 0, before_ref if fresh else total_ref)
        if held > 1:

            def add_more(at, carry, source_ref=source_ref, number=number):
                row = pl.multiple_of(at * group * leaf_rows, SUBLANES)
                add_group(source_ref, row, number + at * group, 0, total_ref)
                return carry

            lax.fori_loop(1, held, add_more, 0)
        number += held * group
    if final:
        for at in range(out_ref.shape[0]):
            out_ref[at : at + 1, :] = lane_sums(total_ref[at * LANES : (at + 1) * LANES, :])


def add_tree(terms):
    while len(terms) > 1:
        terms = [
            terms[i] + terms[i + 1] if i + 1 < len(terms) else terms[i]
            for i in range(0, len(terms), 2)
        ]
    return terms[0]


def lane_spread(block, k):
    return jnp.broadcast_to(block[:, k : k + 1], block.shape)


def row_spread(block, k):
    return jnp.broadcast_to(block[k : k + 1, :], block.shape)


def factor_all(blocks, moments, keep, one, outer):
    count = len(blocks)
    rank = blocks[0][0].shape[1]
    block_count = rank // SUBLANES
    lane_id = lax.broadcasted_iota(jnp.int32, (SUBLANES, rank), 1)
    row_id = lax.broadcasted_iota(jnp.int32, (SUBLANES, rank), 0)
    corner = [None] * count
    factors = [[None] * block_count for _ in range(count)]
    for t in range(block_count):
        panel = t // outer * outer
        end = min(panel + outer, block_count)
        raw = [[[None] * SUBLANES for _ in range(block_count)] for _ in range(count)]
        for i in range(t, end):
            for k in range(SUBLANES):
                for b in range(count):
                    raw[b][i][k] = lane_spread(blocks[b][i], SUBLANES * t + k)
        if t == 0:
            for b in range(count):
                for i in range(block_count):
                    blocks[b][i] = jnp.where(lane_id == 0, moments[b][i], blocks[b][i])
        columns = [[raw[b][t][k] * one for k in range(SUBLANES)] for b in range(count)]
        rows = [blocks[b][t] for b in range(count)]
        done = [None] * count
        for r in range(0, SUBLANES, 2):
            first = row_id == r
            second = row_id == r + 1
            pivot = first | second
            for b in range(count):
                column = columns[b]
                above = column[r]
                beside = column[r + 1]
                aa = row_spread(above, r)
                ab = row_spread(above, r + 1)
                bb = row_spread(beside, r + 1)
                determinant = aa * bb - ab * ab
                inverse = 1.0 / determinant
                root_a = lax.rsqrt(aa)
                root_d = lax.rsqrt(determinant)
                row_a = row_spread(rows[b], r)
                row_b = row_spread(rows[b], r + 1)
                factor_a = row_a * root_a
                factor_b = (row_b * aa - row_a * ab) * (root_a * root_d)
                done[b] = jnp.where(
                    first,
                    factor_a,
                    factor_b if done[b] is None else jnp.where(second, factor_b, done[b]),
                )
                if t == 0 and r == 0:
                    corner[b] = aa * root_a
                if r + 2 < SUBLANES or t + 1 < end:
                    inv_b = bb * inverse
                    inv_ab = ab * inverse
                    inv_a = aa * inverse
                    by_a = above * inv_b - beside * inv_ab
                    by_b = beside * inv_a - above * inv_ab
                    by_a = jnp.where(first, -inv_b, jnp.where(second, inv_ab, by_a))
                    by_b = jnp.where(first, inv_ab, jnp.where(second, -inv_a, by_b))
                    for k in range(r + 2, SUBLANES):
                        column[k] = jnp.where(pivot, 0.0, column[k]) - (
                            by_a * row_spread(column[k], r) + by_b * row_spread(column[k], r + 1)
                        )
                    rows[b] = jnp.where(pivot, 0.0, rows[b]) - (by_a * row_a + by_b * row_b)
        for b in range(count):
            keep(b, t, done[b])
            factors[b][t] = done[b]
            if t + 1 < end:
                weights = [row_spread(rows[b], k) for k in range(SUBLANES)]
                for i in range(t + 1, end):
                    blocks[b][i] = blocks[b][i] - add_tree(
                        [raw[b][i][k] * weights[k] for k in range(SUBLANES)]
                    )
            elif end < block_count:
                upper = jnp.concatenate(factors[b][panel:end], axis=0)
                lower = jnp.transpose(upper)[SUBLANES * end :, :]
                change = jnp.dot(
                    lower, upper, precision=HIGHEST, preferred_element_type=jnp.float32
                )
                for i in range(end, block_count):
                    at = SUBLANES * (i - end)
                    blocks[b][i] = blocks[b][i] - change[at : at + SUBLANES, :]
    return corner


def factor_body(
    gram_ref, moment_ref, held_ref, other_ref, coeffs_ref, top_factor_ref, top_coeffs_ref, *scratch, node_count
):
    upper_ref, one_ref = scratch
    per_device, _, rank = gram_ref.shape
    count = per_device + 1
    block_count = rank // SUBLANES
    one_ref[...] = jnp.ones_like(one_ref)
    folded = held_ref[held_ref.shape[0] - fold_rows(rank) :, :]
    folded = folded + other_ref[other_ref.shape[0] - fold_rows(rank) :, :]
    sources = [(gram_ref[member], moment_ref[member : member + 1, :]) for member in range(per_device)]
    sources.append(unfold(folded))
    blocks = [
        [gram[SUBLANES * i : SUBLANES * (i + 1), :] for i in range(block_count)]
        for gram, _ in sources
    ]
    moments = []
    for _, moment in sources:
        columns = jnp.transpose(jnp.broadcast_to(moment, (rank, rank)))
        moments.append([columns[SUBLANES * i : SUBLANES * (i + 1), :] for i in range(block_count)])

    def keep(b, t, block):
        upper_ref[b, SUBLANES * t : SUBLANES * (t + 1), :] = block

    corner = factor_all(blocks, moments, keep, one_ref[...], 8)
    for member in range(per_device):
        coeffs_ref[member : member + 1, :] = jnp.transpose(upper_ref[member])[0:1, :]
    lower = jnp.transpose(upper_ref[per_device])
    row = lax.broadcasted_iota(jnp.int32, (rank, rank), 0)
    column = lax.broadcasted_iota(jnp.int32, (rank, rank), 1)
    top = jnp.where(row >= column, lower, 0.0)
    top = jnp.where(row == 0, jnp.where(column == 0, corner[per_device][0:1, :], 0.0), top)
    upper_ref[per_device] = top
    share = rank // node_count
    node_index = lax.axis_index("node")
    start = pl.multiple_of(node_index * share, SUBLANES)
    top_factor_ref[0] = upper_ref[per_device, pl.ds(start, share), :]
    mine = lower[0:1, 0:share]
    for node in range(1, node_count):
        mine = jnp.where(node_index == node, lower[0:1, node * share : (node + 1) * share], mine)
    top_coeffs_ref[...] = mine


def body(positions, charges, near_list, near_count, far_sample, proxies, strengths):
    per_device = near_count.shape[0]
    leaf_size = charges.shape[0] // per_device
    rank = far_sample.shape[1]
    node_count = lax.axis_size("node")
    block_total = lax.axis_size("leaf")
    half = node_count // 2
    pieces = leaf_size // LANES
    assert pieces == COORDS
    points_rows = per_device * pieces * COORDS
    f32 = jnp.float32

    def in_hbm(array):
        return pltpu.with_memory_space_constraint(array, pltpu.HBM)

    def across(block, apart):
        return lax.ppermute(block, "node", [(z, z ^ apart) for z in range(node_count)])

    def diagonal(block):
        route = []
        for at in range(block_total):
            for z in range(node_count):
                to = at + 1 if z >= half else at - 1
                if 0 <= to < block_total:
                    route.append((at * node_count + z, to * node_count + (z ^ half)))
        return lax.ppermute(block, ("leaf", "node"), route)

    payload, target, centre, gram, moment = pl.pallas_call(
        gram_body,
        out_shape=(
            jax.ShapeDtypeStruct((points_rows + fold_rows(rank), rank), f32),
            jax.ShapeDtypeStruct((per_device * leaf_size, SUBLANES * len(PART_PAIRS)), jnp.bfloat16),
            jax.ShapeDtypeStruct((SUBLANES, LANES), f32),
            jax.ShapeDtypeStruct((per_device, rank, rank), f32),
            jax.ShapeDtypeStruct((per_device, rank), f32),
        ),
        in_specs=[HBM_SPEC] * 5,
        out_specs=(VMEM_SPEC,) * 5,
        scratch_shapes=[
            pltpu.VMEM(positions.shape, f32),
            pltpu.VMEM((per_device * pieces, LANES), f32),
            pltpu.VMEM(far_sample.shape, f32),
            pltpu.VMEM((3, per_device, rank), f32),
            pltpu.VMEM(strengths.shape, f32),
            pltpu.SemaphoreType.DMA((4 + per_device,)),
        ],
        compiler_params=pltpu.CompilerParams(vmem_limit_bytes=VMEM_LIMIT),
        name="gram",
    )(
        in_hbm(positions),
        in_hbm(charges.reshape(per_device * pieces, LANES)),
        in_hbm(far_sample),
        in_hbm(proxies.transpose(1, 0, 2)),
        in_hbm(strengths),
    )

    totals = jax.ShapeDtypeStruct((per_device * leaf_size, LANES), f32)
    numbers = 3 * half * per_device
    params = pltpu.CompilerParams(vmem_limit_bytes=VMEM_LIMIT)
    work = pl.CostEstimate(flops=1 << 31, bytes_accessed=1 << 20, transcendentals=0)
    other_half = across(payload, half)
    side = diagonal(payload)
    total, flags = pl.pallas_call(
        functools.partial(own_body, node_count=node_count),
        out_shape=(totals, jax.ShapeDtypeStruct((numbers, SUBLANES, LANES), f32)),
        in_specs=[HBM_SPEC] * 2 + [VMEM_SPEC] * 3,
        out_specs=(VMEM_SPEC,) * 2,
        scratch_shapes=[
            pltpu.VMEM(near_list.shape, jnp.int32),
            pltpu.SMEM(near_count.shape, jnp.int32),
            pltpu.SemaphoreType.DMA((2,)),
        ],
        compiler_params=params,
        cost_estimate=work,
        name="near_own",
    )(in_hbm(near_list), in_hbm(near_count), payload, target, centre)
    held = pl.pallas_call(
        functools.partial(merge_body, rows=points_rows),
        out_shape=jax.ShapeDtypeStruct((3 * points_rows + fold_rows(rank), rank), f32),
        in_specs=[VMEM_SPEC] * 3,
        out_specs=VMEM_SPEC,
        name="merge",
    )(payload, other_half, side)

    def near(first, last, sources, final):
        return pl.pallas_call(
            functools.partial(
                near_body, first=first, last=last, source_count=len(sources), final=final
            ),
            out_shape=jax.ShapeDtypeStruct((per_device * pieces, LANES), f32) if final else totals,
            in_specs=[VMEM_SPEC] * (4 + len(sources)),
            out_specs=VMEM_SPEC,
            scratch_shapes=[pltpu.VMEM(totals.shape, f32)] if final else [],
            input_output_aliases={} if final else {3: 0},
            compiler_params=params,
            cost_estimate=work,
            name="near_rest" if final else "near_first",
        )(flags, centre, target, total, *sources)

    arrived = []
    apart = 1
    while apart < half:
        arrived.append(across(held, apart))
        if apart == 1:
            total = near(per_device, 3 * per_device, [held], False)
        if 2 * apart < half:
            rows = held.shape[0] - fold_rows(rank)
            held = jnp.concatenate(
                [held[:rows], arrived[-1][:rows], held[rows:] + arrived[-1][rows:]]
            )
        apart *= 2
    potential = near(3 * per_device, numbers, arrived, True)

    share = rank // node_count
    coeffs, top_factor, top_coeffs = pl.pallas_call(
        functools.partial(factor_body, node_count=node_count),
        out_shape=(
            jax.ShapeDtypeStruct((per_device, rank), f32),
            jax.ShapeDtypeStruct((1, share, rank), f32),
            jax.ShapeDtypeStruct((1, share), f32),
        ),
        in_specs=[VMEM_SPEC] * 4,
        out_specs=(VMEM_SPEC,) * 3,
        scratch_shapes=[
            pltpu.VMEM((per_device + 1, rank, rank), f32),
            pltpu.VMEM((SUBLANES, rank), f32),
        ],
        compiler_params=pltpu.CompilerParams(vmem_limit_bytes=VMEM_LIMIT),
        name="factors",
    )(gram, moment, held, arrived[-1])
    return (potential.reshape(-1), coeffs, top_factor, top_coeffs)


def solution(mesh):
    in_specs = (
        P(None, ("leaf", "node")),
        P(("leaf", "node")),
        P(("leaf", "node"), None),
        P(("leaf", "node")),
        P(("leaf", "node"), None),
        P(("leaf", "node"), None, None),
        P(("leaf", "node"), None),
    )
    out_specs = (
        P(("leaf", "node")),
        P(("leaf", "node"), None),
        P("leaf", "node", None),
        P("leaf", "node"),
    )
    return jax.shard_map(body, mesh=mesh, in_specs=in_specs, out_specs=out_specs, check_vma=False)
```

profile of v0, /device:TPU:0, one launch (start us, length us, event | category | flops | bytes accessed | tf_op | source)
XLA Modules:
  0.0 29.2 jit_solution(17434138208060279192)
XLA Ops:
  0.6 2.5 %gram.1 = (f32[104,128]{1,0:T(8,128)S(1)}, bf16[1024,64]{1,0:T(8,128)(2,1)S(1)}, f32[8,128]{1,0:T(8,128)S(1)}, f32[2,128,128]{2,1,0:T(8,128)S(1)}, f32[2,128]{1,0:T(2,128)S(1)}) custom-call(f32[3,1024]{1,0:T(4,128)} %positions_hbm.1, f32[8,128]{1,0:T(8,128)} %bitcast.3, f32[1024,128]{1,0:T(8,128)} %far_hbm.1, f32[3,2,128]{2,1,0:T(2,128)} %bitcast.4, ...), custom_call_target="tpu_custom_call" | custom-call | tf_op jit(solution)/shard_map/gram/pallas_call | solution.py:493
  3.1 0.0 copy-start.2
  3.1 0.7 %collective-permute-start.1 = (f32[104,128]{1,0:T(8,128)S(1)}, f32[104,128]{1,0:T(8,128)S(1)}, u32[]{:S(2)}, u32[]{:S(2)}) collective-permute-start(f32[104,128]{1,0:T(8,128)S(1)} %get-tuple-element.14.payload_ref), channel_id=1, source_target_pairs={{2,4},{3,5},{4,2},{5,3},{6,8},{7,9},{8,6},{9,7},{10,12},{11,13},{1... | collective-permute-start | bytes 159752 | tf_op jit(solution)/shard_map/ppermute | solution.py:491
  3.8 5.4 %collective-permute-start = (f32[104,128]{1,0:T(8,128)S(1)}, f32[104,128]{1,0:T(8,128)S(1)}, u32[]{:S(2)}, u32[]{:S(2)}) collective-permute-start(f32[104,128]{1,0:T(8,128)S(1)} %get-tuple-element.14.payload_ref), channel_id=1, source_target_pairs={{0,2},{1,3},{2,0},{3,1},{4,6},{5,7},{6,4},{7,5},{8,10},{9,11},{10,... | collective-permute-start | bytes 159752 | tf_op jit(solution)/shard_map/ppermute | solution.py:482
  9.1 1.5 %near_own.1 = (f32[1024,128]{1,0:T(8,128)S(1)}, f32[12,8,128]{2,1,0:T(8,128)S(1)}) custom-call(s32[2,11]{1,0:T(2,128)} %list_hbm.1, s32[2]{0:T(128)} %count_hbm.1, f32[104,128]{1,0:T(8,128)S(1)} %get-tuple-element.14.payload_ref, bf16[1024,64]{1,0:T(8,128)(2,1)S(1)} %get-tuple-element.15.target_ref.refs_2_, f32[8,128]{1,0:T(8,128)S(1)} %get-tuple-element.16.centre_ref.refs_1_), custom_call_target="tpu_custom_call" | custom-call | flops 2147483648 | bytes 1048576 | tf_op jit(solution)/shard_map/near_own/pallas_call | solution.py:528
  10.6 0.0 copy-done.2
  10.7 0.0 collective-permute-done.1.side_ref
  10.7 0.0 copy-start.3
  10.7 3.8 %collective-permute-done.other_ref = f32[104,128]{1,0:T(8,128)S(1)} collective-permute-done((f32[104,128]{1,0:T(8,128)S(1)}, f32[104,128]{1,0:T(8,128)S(1)}, u32[]{:S(2)}, u32[]{:S(2)}) %collective-permute-start) | collective-permute-done | bytes 53280 | tf_op jit(solution)/shard_map/ppermute | solution.py:482
  14.5 0.0 copy-done.3
  14.5 0.0 copy-start.4
  14.5 0.6 %copy-done.4 = f32[104,128]{1,0:T(8,128)} copy-done((f32[104,128]{1,0:T(8,128)}, f32[104,128]{1,0:T(8,128)S(1)}, u32[]{:S(2)}) %copy-start.4) | copy-done | bytes 53272
  15.1 1.5 %merge.1.refs_4_.held_ref = f32[168,128]{1,0:T(8,128)} custom-call(f32[104,128]{1,0:T(8,128)} %copy-done.2, f32[104,128]{1,0:T(8,128)} %copy-done.4, f32[104,128]{1,0:T(8,128)} %copy-done.3), custom_call_target="tpu_custom_call" | custom-call | tf_op jit(solution)/shard_map/merge/pallas_call | solution.py:542
  16.6 0.0 collective-permute-start.2
  16.6 0.0 copy-start
  16.6 0.9 %copy-done = f32[168,128]{1,0:T(8,128)S(1)} copy-done((f32[168,128]{1,0:T(8,128)S(1)}, f32[168,128]{1,0:T(8,128)}, u32[]{:S(2)}) %copy-start) | copy-done | bytes 86040
  17.6 1.3 %near_first.1.refs_3_ = f32[1024,128]{1,0:T(8,128)S(1)} custom-call(f32[12,8,128]{2,1,0:T(8,128)S(1)} %get-tuple-element.17.refs_0_, f32[8,128]{1,0:T(8,128)S(1)} %get-tuple-element.16.centre_ref.refs_1_, bf16[1024,64]{1,0:T(8,128)(2,1)S(1)} %get-tuple-element.15.target_ref.refs_2_, ...), custom_call_target="tpu_custom_call", output_to_operand_aliasing={{}: (3, {})} | custom-call | flops 2147483648 | bytes 1048576 | tf_op jit(solution)/shard_map/near_first/pallas_call | solution.py:551
  18.8 0.0 copy-start.1
  18.8 2.9 %collective-permute-done.2.refs_4_.other_ref = f32[168,128]{1,0:T(8,128)S(1)} collective-permute-done((f32[168,128]{1,0:T(8,128)}, f32[168,128]{1,0:T(8,128)S(1)}, u32[]{:S(2)}, u32[]{:S(2)}) %collective-permute-start.2) | collective-permute-done | bytes 86048 | tf_op jit(solution)/shard_map/ppermute | solution.py:482
  21.7 2.6 %near_rest.1 = f32[8,128]{1,0:T(8,128)} custom-call(f32[12,8,128]{2,1,0:T(8,128)S(1)} %get-tuple-element.17.refs_0_, f32[8,128]{1,0:T(8,128)S(1)} %get-tuple-element.16.centre_ref.refs_1_, bf16[1024,64]{1,0:T(8,128)(2,1)S(1)} %get-tuple-element.15.target_ref.refs_2_, f32[1024,128]{1,0:T(8,128)S(1)} %near_first.1.refs_3_, ...), custom_call_target="tpu_custom_call" | custom-call | flops 2147483648 | bytes 1048576 | tf_op jit(solution)/shard_map/near_rest/pallas_call | solution.py:551
  24.4 0.0 copy-done.1
  24.4 4.9 %factors.1 = (f32[2,128]{1,0:T(2,128)}, f32[1,32,128]{2,1,0:T(8,128)}, f32[1,32]{1,0:T(1,128)}) custom-call(f32[2,128,128]{2,1,0:T(8,128)S(1)} %get-tuple-element.19.gram_ref, f32[2,128]{1,0:T(2,128)S(1)} %get-tuple-element.20.moment_ref, f32[168,128]{1,0:T(8,128)S(1)} %copy-done.1, f32[168,128]{1,0:T(8,128)S(1)} %collective-permute-done.2.refs_4_.other_ref), custom_call_target="tpu_custom_call" | custom-call | tf_op jit(solution)/shard_map/factors/pallas_call | solution.py:580
Async XLA Ops:
  3.1 7.6 %copy-start.2 = (f32[104,128]{1,0:T(8,128)}, f32[104,128]{1,0:T(8,128)S(1)}, u32[]{:S(2)}) copy-start(f32[104,128]{1,0:T(8,128)S(1)} %get-tuple-element.14.payload_ref) | copy-start | bytes 159748
  3.1 7.6 %collective-permute-start.1 = (f32[104,128]{1,0:T(8,128)S(1)}, f32[104,128]{1,0:T(8,128)S(1)}, u32[]{:S(2)}, u32[]{:S(2)}) collective-permute-start(f32[104,128]{1,0:T(8,128)S(1)} %get-tuple-element.14.payload_ref), channel_id=1, source_target_pairs={{2,4},{3,5},{4,2},{5,3},{6,8},{7,9},{8,6},{9,7},{10,12},{11,13},{1... | collective-permute-start | bytes 159752 | tf_op jit(solution)/shard_map/ppermute | solution.py:491
  3.8 10.7 %collective-permute-start = (f32[104,128]{1,0:T(8,128)S(1)}, f32[104,128]{1,0:T(8,128)S(1)}, u32[]{:S(2)}, u32[]{:S(2)}) collective-permute-start(f32[104,128]{1,0:T(8,128)S(1)} %get-tuple-element.14.payload_ref), channel_id=1, source_target_pairs={{0,2},{1,3},{2,0},{3,1},{4,6},{5,7},{6,4},{7,5},{8,10},{9,11},{10,... | collective-permute-start | bytes 159752 | tf_op jit(solution)/shard_map/ppermute | solution.py:482
  10.7 3.9 %copy-start.3 = (f32[104,128]{1,0:T(8,128)}, f32[104,128]{1,0:T(8,128)S(1)}, u32[]{:S(2)}) copy-start(f32[104,128]{1,0:T(8,128)S(1)} %collective-permute-done.1.side_ref) | copy-start | bytes 159748
  14.5 0.6 %copy-start.4 = (f32[104,128]{1,0:T(8,128)}, f32[104,128]{1,0:T(8,128)S(1)}, u32[]{:S(2)}) copy-start(f32[104,128]{1,0:T(8,128)S(1)} %collective-permute-done.other_ref) | copy-start | bytes 159748
  16.6 5.1 %collective-permute-start.2 = (f32[168,128]{1,0:T(8,128)}, f32[168,128]{1,0:T(8,128)S(1)}, u32[]{:S(2)}, u32[]{:S(2)}) collective-permute-start(f32[168,128]{1,0:T(8,128)} %merge.1.refs_4_.held_ref), channel_id=1, source_target_pairs={{0,1},{1,0},{2,3},{3,2},{4,5},{5,4},{6,7},{7,6},{8,9},{9,8},{10,11... | collective-permute-start | bytes 258056 | tf_op jit(solution)/shard_map/ppermute | solution.py:482
  16.6 0.9 %copy-start = (f32[168,128]{1,0:T(8,128)S(1)}, f32[168,128]{1,0:T(8,128)}, u32[]{:S(2)}) copy-start(f32[168,128]{1,0:T(8,128)} %merge.1.refs_4_.held_ref) | copy-start | bytes 258052
  18.8 5.5 %copy-start.1 = (f32[168,128]{1,0:T(8,128)S(1)}, f32[168,128]{1,0:T(8,128)}, u32[]{:S(2)}) copy-start(f32[168,128]{1,0:T(8,128)} %merge.1.refs_4_.held_ref) | copy-start | bytes 258052
where the time goes:
time: 29.5 us; the launch traced here: 29.2 us
  Pallas kernels  14.2 us (48%)
  waiting for transfers between devices  6.75 us (23%)
  starting transfers between devices  6.03 us (20%)
  local copies, waits for them, and re-layouts  1.54 us (5%)
  between operations  0.71 us (2%)
    ppermute x2, waiting for transfers between devices, across(): lax.ppermute(block, 'node', [(z, z ^ apart) for z in range(node_count)])  6.74 us
    ppermute x2, starting transfers between devices, across(): lax.ppermute(block, 'node', [(z, z ^ apart) for z in range(node_count)])  5.36 us
    pallas_call x1, Pallas kernels, body(): pl.pallas_call(functools.partial(factor_body, node_count=node_count), out...  4.86 us
    pallas_call x2, Pallas kernels, near(): pl.pallas_call(functools.partial(near_body, first=first, last=last, sourc...  3.89 us
    pallas_call x1, Pallas kernels, body(): pl.pallas_call(gram_body, out_shape=(jax.ShapeDtypeStruct((points_rows +...  2.45 us
    unnamed x10, local copies, waits for them, and re-layouts  1.54 us
    pallas_call x1, Pallas kernels, body(): pl.pallas_call(functools.partial(merge_body, rows=points_rows), out_shape...  1.51 us
    pallas_call x1, Pallas kernels, body(): pl.pallas_call(functools.partial(own_body, node_count=node_count), out_sh...  1.5 us
  transfers between devices with their start and end apart: 3, of which 2 were waited for; matrix products, arithmetic and copies ran while one was open for 0% of the time, Pallas kernels for 9%

commit v1 on v0

--- a/solution.py
+++ b/solution.py
@@ -14,7 +14,7 @@
 HBM_SPEC = pl.BlockSpec(memory_space=pltpu.HBM)
 LANES = 128
 COORDS = 4
-VMEM_LIMIT = 24 << 20
+VMEM_LIMIT = 16 << 20
 PART_PAIRS = ((0, 0), (0, 1), (1, 0), (1, 1), (0, 2), (2, 0), (1, 2), (2, 1))
 
 
@@ -103,6 +103,7 @@
     far_hbm,
     proxies_hbm,
     strengths_hbm,
+    points_ref,
     payload_ref,
     target_ref,
     centre_ref,
@@ -150,8 +151,8 @@
         for piece in range(pieces):
             at = (member * pieces + piece) * COORDS
             lanes = slice(span.start + piece * LANES, span.start + (piece + 1) * LANES)
-            payload_ref[at : at + 3, :] = positions_ref[:, lanes]
-            payload_ref[at + 3 : at + 4, :] = charges_ref[at // COORDS : at // COORDS + 1, :]
+            points_ref[at : at + 3, :] = positions_ref[:, lanes]
+            points_ref[at + 3 : at + 4, :] = charges_ref[at // COORDS : at // COORDS + 1, :]
         target = jnp.transpose(target_factor(shifted[:, span])).astype(jnp.bfloat16)
         target_ref[span, :] = target
         proxies = jnp.concatenate([proxies_ref[c, member : member + 1, :] for c in range(3)], axis=0)
@@ -172,6 +173,7 @@
         total_gram = total_gram + both[:rank, :]
         total_moment = total_moment + both[rank : rank + 1, :]
     points_rows = per_device * pieces * COORDS
+    payload_ref[:points_rows, :] = points_ref[...]
     payload_ref[points_rows:, :] = fold(total_gram, total_moment)
 
 
@@ -280,12 +282,11 @@
     held_ref[3 * rows :, :] = payload_ref[rows:, :] + other_ref[rows:, :]
 
 
-def near_body(*refs, first, last, source_count, final):
+def near_body(*refs, first, last, leaf_size, source_count, final):
     flags_ref, centre_ref, target_ref, before_ref = refs[:4]
     source_refs = refs[4 : 4 + source_count]
     out_ref = refs[4 + source_count]
     total_ref = refs[5 + source_count] if final else out_ref
-    leaf_size = LANES * COORDS
     per_device = target_ref.shape[0] // leaf_size
     leaf_rows = leaf_size // LANES * COORDS
     group = 3 * per_device
@@ -471,7 +472,6 @@
     block_total = lax.axis_size("leaf")
     half = node_count // 2
     pieces = leaf_size // LANES
-    assert pieces == COORDS
     points_rows = per_device * pieces * COORDS
     f32 = jnp.float32
 
@@ -490,9 +490,10 @@
                     route.append((at * node_count + z, to * node_count + (z ^ half)))
         return lax.ppermute(block, ("leaf", "node"), route)
 
-    payload, target, centre, gram, moment = pl.pallas_call(
+    points, payload, target, centre, gram, moment = pl.pallas_call(
         gram_body,
         out_shape=(
+            jax.ShapeDtypeStruct((points_rows, LANES), f32),
             jax.ShapeDtypeStruct((points_rows + fold_rows(rank), rank), f32),
             jax.ShapeDtypeStruct((per_device * leaf_size, SUBLANES * len(PART_PAIRS)), jnp.bfloat16),
             jax.ShapeDtypeStruct((SUBLANES, LANES), f32),
@@ -500,7 +501,7 @@
             jax.ShapeDtypeStruct((per_device, rank), f32),
         ),
         in_specs=[HBM_SPEC] * 5,
-        out_specs=(VMEM_SPEC,) * 5,
+        out_specs=(VMEM_SPEC,) * 6,
         scratch_shapes=[
             pltpu.VMEM(positions.shape, f32),
             pltpu.VMEM((per_device * pieces, LANES), f32),
@@ -524,7 +525,7 @@
     params = pltpu.CompilerParams(vmem_limit_bytes=VMEM_LIMIT)
     work = pl.CostEstimate(flops=1 << 31, bytes_accessed=1 << 20, transcendentals=0)
     other_half = across(payload, half)
-    side = diagonal(payload)
+    side = diagonal(points)
     total, flags = pl.pallas_call(
         functools.partial(own_body, node_count=node_count),
         out_shape=(totals, jax.ShapeDtypeStruct((numbers, SUBLANES, LANES), f32)),
@@ -544,13 +545,19 @@
         out_shape=jax.ShapeDtypeStruct((3 * points_rows + fold_rows(rank), rank), f32),
         in_specs=[VMEM_SPEC] * 3,
         out_specs=VMEM_SPEC,
+        compiler_params=params,
         name="merge",
     )(payload, other_half, side)
 
     def near(first, last, sources, final):
         return pl.pallas_call(
             functools.partial(
-                near_body, first=first, last=last, source_count=len(sources), final=final
+                near_body,
+                first=first,
+                last=last,
+                leaf_size=leaf_size,
+                source_count=len(sources),
+                final=final,
             ),
             out_shape=jax.ShapeDtypeStruct((per_device * pieces, LANES), f32) if final else totals,
             in_specs=[VMEM_SPEC] * (4 + len(sources)),

time: 29.5 us -> 25.9 us (0.88)
  the two profiles are of different devices: /device:TPU:0 before, /device:TPU:2 now
where the time goes in v1:
time: 25.9 us; the launch traced here: 25.6 us
  Pallas kernels  12.7 us (49%)
  waiting for transfers between devices  7.05 us (27%)
  starting transfers between devices  5.18 us (20%)
  between operations  0.67 us (3%)
    ppermute x2, waiting for transfers between devices, across(): lax.ppermute(block, 'node', [(z, z ^ apart) for z in range(node_count)])  6.22 us
    pallas_call x1, Pallas kernels, body(): pl.pallas_call(functools.partial(factor_body, node_count=node_count), out...  4.86 us
    ppermute x1, starting transfers between devices, diagonal(): return lax.ppermute(block, ('leaf', 'node'), route)  3.91 us
    pallas_call x2, Pallas kernels, near(): pl.pallas_call(functools.partial(near_body, first=first, last=last, leaf_...  3.89 us
    pallas_call x1, Pallas kernels, body(): pl.pallas_call(gram_body, out_shape=(jax.ShapeDtypeStruct((points_rows, L...  2.45 us
    pallas_call x1, Pallas kernels, body(): pl.pallas_call(functools.partial(own_body, node_count=node_count), out_sh...  1.5 us
    ppermute x2, starting transfers between devices, across(): lax.ppermute(block, 'node', [(z, z ^ apart) for z in range(node_count)])  1.27 us
    ppermute x1, waiting for transfers between devices, diagonal(): return lax.ppermute(block, ('leaf', 'node'), route)  0.83 us
  transfers between devices with their start and end apart: 3, of which 3 were waited for; matrix products, arithmetic and copies ran while one was open for 0% of the time, Pallas kernels for 11%

profile of v1, /device:TPU:2, one launch (start us, length us, event | category | flops | bytes accessed | tf_op | source)
XLA Modules:
  0.0 25.6 jit_solution(17371089720606333535)
XLA Ops:
  0.6 2.5 %gram.1 = (f32[32,128]{1,0:T(8,128)S(1)}, f32[104,128]{1,0:T(8,128)S(1)}, bf16[1024,64]{1,0:T(8,128)(2,1)S(1)}, f32[8,128]{1,0:T(8,128)S(1)}, f32[2,128,128]{2,1,0:T(8,128)S(1)}, /*index=5*/f32[2,128]{1,0:T(2,128)S(1)}) custom-call(f32[3,1024]{1,0:T(4,128)} %positions_hbm.1, f32[8,128]{1,0:T(8,128)} %bitcast.3, f32[1024,128]{1,0:T(8,128)} %far_hbm.1, ...), custom_call_target="tpu_custom_call" | custom-call | tf_op jit(solution)/shard_map/gram/pallas_call | solution.py:493
  3.1 3.9 %collective-permute-start.1 = (f32[32,128]{1,0:T(8,128)S(1)}, f32[32,128]{1,0:T(8,128)S(1)}, u32[]{:S(2)}, u32[]{:S(2)}) collective-permute-start(f32[32,128]{1,0:T(8,128)S(1)} %get-tuple-element.20), channel_id=1, source_target_pairs={{2,4},{3,5},{4,2},{5,3},{6,8},{7,9},{8,6},{9,7},{10,12},{11,13},{1... | collective-permute-start | bytes 49160 | tf_op jit(solution)/shard_map/ppermute | solution.py:491
  7.0 0.7 %collective-permute-start = (f32[104,128]{1,0:T(8,128)S(1)}, f32[104,128]{1,0:T(8,128)S(1)}, u32[]{:S(2)}, u32[]{:S(2)}) collective-permute-start(f32[104,128]{1,0:T(8,128)S(1)} %get-tuple-element.15.payload_ref), channel_id=1, source_target_pairs={{0,2},{1,3},{2,0},{3,1},{4,6},{5,7},{6,4},{7,5},{8,10},{9,11},{10,... | collective-permute-start | bytes 159752 | tf_op jit(solution)/shard_map/ppermute | solution.py:482
  7.7 1.5 %near_own.1 = (f32[1024,128]{1,0:T(8,128)S(1)}, f32[12,8,128]{2,1,0:T(8,128)S(1)}) custom-call(s32[2,11]{1,0:T(2,128)} %list_hbm.1, s32[2]{0:T(128)} %count_hbm.1, f32[104,128]{1,0:T(8,128)S(1)} %get-tuple-element.15.payload_ref, bf16[1024,64]{1,0:T(8,128)(2,1)S(1)} %get-tuple-element.16.target_ref.refs_2_, f32[8,128]{1,0:T(8,128)S(1)} %get-tuple-element.17.centre_ref.refs_1_), custom_call_target="tpu_custom_call" | custom-call | flops 2147483648 | bytes 1048576 | tf_op jit(solution)/shard_map/near_own/pallas_call | solution.py:529
  9.2 0.8 %collective-permute-done.1.side_ref = f32[32,128]{1,0:T(8,128)S(1)} collective-permute-done((f32[32,128]{1,0:T(8,128)S(1)}, f32[32,128]{1,0:T(8,128)S(1)}, u32[]{:S(2)}, u32[]{:S(2)}) %collective-permute-start.1) | collective-permute-done | bytes 16416 | tf_op jit(solution)/shard_map/ppermute | solution.py:491
  10.0 3.5 %collective-permute-done.other_ref = f32[104,128]{1,0:T(8,128)S(1)} collective-permute-done((f32[104,128]{1,0:T(8,128)S(1)}, f32[104,128]{1,0:T(8,128)S(1)}, u32[]{:S(2)}, u32[]{:S(2)}) %collective-permute-start) | collective-permute-done | bytes 53280 | tf_op jit(solution)/shard_map/ppermute | solution.py:482
  13.6 0.6 %collective-permute-start.2 = (f32[168,128]{1,0:T(8,128)S(1)}, f32[168,128]{1,0:T(8,128)S(1)}, u32[]{:S(2)}, u32[]{:S(2)}) collective-permute-start(f32[168,128]{1,0:T(8,128)S(1)} %merge.1.refs_4_.held_ref), channel_id=1, source_target_pairs={{0,1},{1,0},{2,3},{3,2},{4,5},{5,4},{6,7},{7,6},{8,9},{9,8},{10,11... | collective-permute-start | bytes 258056 | tf_op jit(solution)/shard_map/ppermute | solution.py:482
  14.2 1.3 %near_first.1.refs_3_ = f32[1024,128]{1,0:T(8,128)S(1)} custom-call(f32[12,8,128]{2,1,0:T(8,128)S(1)} %get-tuple-element.18.refs_0_, f32[8,128]{1,0:T(8,128)S(1)} %get-tuple-element.17.centre_ref.refs_1_, bf16[1024,64]{1,0:T(8,128)(2,1)S(1)} %get-tuple-element.16.target_ref.refs_2_, ...), custom_call_target="tpu_custom_call", output_to_operand_aliasing={{}: (3, {})} | custom-call | flops 2147483648 | bytes 1048576 | tf_op jit(solution)/shard_map/near_first/pallas_call | solution.py:553
  15.4 2.7 %collective-permute-done.2.refs_4_.other_ref = f32[168,128]{1,0:T(8,128)S(1)} collective-permute-done((f32[168,128]{1,0:T(8,128)S(1)}, f32[168,128]{1,0:T(8,128)S(1)}, u32[]{:S(2)}, u32[]{:S(2)}) %collective-permute-start.2) | collective-permute-done | bytes 86048 | tf_op jit(solution)/shard_map/ppermute | solution.py:482
  18.1 2.6 %near_rest.1 = f32[8,128]{1,0:T(8,128)} custom-call(f32[12,8,128]{2,1,0:T(8,128)S(1)} %get-tuple-element.18.refs_0_, f32[8,128]{1,0:T(8,128)S(1)} %get-tuple-element.17.centre_ref.refs_1_, bf16[1024,64]{1,0:T(8,128)(2,1)S(1)} %get-tuple-element.16.target_ref.refs_2_, f32[1024,128]{1,0:T(8,128)S(1)} %near_first.1.refs_3_, ...), custom_call_target="tpu_custom_call" | custom-call | flops 2147483648 | bytes 1048576 | tf_op jit(solution)/shard_map/near_rest/pallas_call | solution.py:553
  20.8 4.9 %factors.1 = (f32[2,128]{1,0:T(2,128)}, f32[1,32,128]{2,1,0:T(8,128)}, f32[1,32]{1,0:T(1,128)}) custom-call(f32[2,128,128]{2,1,0:T(8,128)S(1)} %get-tuple-element.21.gram_ref, f32[2,128]{1,0:T(2,128)S(1)} %get-tuple-element.22.moment_ref, f32[168,128]{1,0:T(8,128)S(1)} %merge.1.refs_4_.held_ref, f32[168,128]{1,0:T(8,128)S(1)} %collective-permute-done.2.refs_4_.other_ref), custom_call_target="tpu_custom_call" | custom-call | tf_op jit(solution)/shard_map/factors/pallas_call | solution.py:587
  (1 shorter events, 0.0 us)
Async XLA Ops:
  3.1 6.9 %collective-permute-start.1 = (f32[32,128]{1,0:T(8,128)S(1)}, f32[32,128]{1,0:T(8,128)S(1)}, u32[]{:S(2)}, u32[]{:S(2)}) collective-permute-start(f32[32,128]{1,0:T(8,128)S(1)} %get-tuple-element.20), channel_id=1, source_target_pairs={{2,4},{3,5},{4,2},{5,3},{6,8},{7,9},{8,6},{9,7},{10,12},{11,13},{1... | collective-permute-start | bytes 49160 | tf_op jit(solution)/shard_map/ppermute | solution.py:491
  7.0 6.5 %collective-permute-start = (f32[104,128]{1,0:T(8,128)S(1)}, f32[104,128]{1,0:T(8,128)S(1)}, u32[]{:S(2)}, u32[]{:S(2)}) collective-permute-start(f32[104,128]{1,0:T(8,128)S(1)} %get-tuple-element.15.payload_ref), channel_id=1, source_target_pairs={{0,2},{1,3},{2,0},{3,1},{4,6},{5,7},{6,4},{7,5},{8,10},{9,11},{10,... | collective-permute-start | bytes 159752 | tf_op jit(solution)/shard_map/ppermute | solution.py:482
  13.6 4.6 %collective-permute-start.2 = (f32[168,128]{1,0:T(8,128)S(1)}, f32[168,128]{1,0:T(8,128)S(1)}, u32[]{:S(2)}, u32[]{:S(2)}) collective-permute-start(f32[168,128]{1,0:T(8,128)S(1)} %merge.1.refs_4_.held_ref), channel_id=1, source_target_pairs={{0,1},{1,0},{2,3},{3,2},{4,5},{5,4},{6,7},{7,6},{8,9},{9,8},{10,11... | collective-permute-start | bytes 258056 | tf_op jit(solution)/shard_map/ppermute | solution.py:482

commit v2 on v1

--- a/solution.py
+++ b/solution.py
@@ -282,16 +282,14 @@
     held_ref[3 * rows :, :] = payload_ref[rows:, :] + other_ref[rows:, :]
 
 
-def near_body(*refs, first, last, leaf_size, source_count, final):
+def near_body(*refs, first, last, leaf_size, source_count):
     flags_ref, centre_ref, target_ref, before_ref = refs[:4]
     source_refs = refs[4 : 4 + source_count]
-    out_ref = refs[4 + source_count]
-    total_ref = refs[5 + source_count] if final else out_ref
+    total_ref = refs[4 + source_count]
     per_device = target_ref.shape[0] // leaf_size
     leaf_rows = leaf_size // LANES * COORDS
     group = 3 * per_device
     centre = centre_ref[...]
-    fresh = True
 
     def add_group(source_ref, row, number, skip, before_ref):
         items = [
@@ -302,11 +300,11 @@
         add_sources(total_ref, before_ref, target_ref, items, flags, per_device, leaf_size)
 
     number = first // group * group
+    before = before_ref
     for source_ref in source_refs:
-        held = (min(last - number, source_ref.shape[0] // leaf_rows)) // group
-        if source_ref is not source_refs[0]:
-            fresh = False
-        add_group(source_ref, 0, number, first % group if fresh else 0, before_ref if fresh else total_ref)
+        held = min(last - number, source_ref.shape[0] // leaf_rows) // group
+        add_group(source_ref, 0, number, first % group if before is before_ref else 0, before)
+        before = total_ref
         if held > 1:
 
             def add_more(at, carry, source_ref=source_ref, number=number):
@@ -316,9 +314,32 @@
 
             lax.fori_loop(1, held, add_more, 0)
         number += held * group
-    if final:
-        for at in range(out_ref.shape[0]):
-            out_ref[at : at + 1, :] = lane_sums(total_ref[at * LANES : (at + 1) * LANES, :])
+
+
+def near_steps(
+    total_ref, out_ref, factor_ref, charge_ref, flags_ref, target_ref, first, leaf_size
+):
+    count = factor_ref.shape[0]
+    per_device = target_ref.shape[0] // leaf_size
+    pieces = leaf_size // LANES
+
+    def add(at, leaf):
+        rows = slice(at * LANES, (at + 1) * LANES)
+        member = at // pieces
+        flag = flags_ref[first + leaf][member : member + 1, :]
+        weight = charge_ref[leaf][0:1, :] * jnp.concatenate([flag] * pieces, axis=1)
+        term = lax.rsqrt(squares(target_ref[rows, :], factor_ref[leaf])) * weight
+        total_ref[rows, :] += add_tree(
+            [term[:, low : low + LANES] for low in range(0, leaf_size, LANES)]
+        )
+
+    def finish(at):
+        out_ref[at : at + 1, :] = lane_sums(total_ref[at * LANES : (at + 1) * LANES, :])
+
+    steps = []
+    for at in range(per_device * pieces):
+        steps += [functools.partial(add, at, leaf) for leaf in range(count)]
+    return steps + [functools.partial(finish, at) for at in range(per_device * pieces)]
 
 
 def add_tree(terms):
@@ -338,7 +359,7 @@
     return jnp.broadcast_to(block[k : k + 1, :], block.shape)
 
 
-def factor_all(blocks, moments, keep, one, outer):
+def factor_all(blocks, moments, keep, one, outer, steps):
     count = len(blocks)
     rank = blocks[0][0].shape[1]
     block_count = rank // SUBLANES
@@ -346,6 +367,8 @@
     row_id = lax.broadcasted_iota(jnp.int32, (SUBLANES, rank), 0)
     corner = [None] * count
     factors = [[None] * block_count for _ in range(count)]
+    places = block_count * SUBLANES // 2
+    place = 0
     for t in range(block_count):
         panel = t // outer * outer
         end = min(panel + outer, block_count)
@@ -362,6 +385,9 @@
         rows = [blocks[b][t] for b in range(count)]
         done = [None] * count
         for r in range(0, SUBLANES, 2):
+            for step in steps[place * len(steps) // places : (place + 1) * len(steps) // places]:
+                step()
+            place += 1
             first = row_id == r
             second = row_id == r + 1
             pivot = first | second
@@ -388,18 +414,17 @@
                 if t == 0 and r == 0:
                     corner[b] = aa * root_a
                 if r + 2 < SUBLANES or t + 1 < end:
-                    inv_b = bb * inverse
-                    inv_ab = ab * inverse
-                    inv_a = aa * inverse
-                    by_a = above * inv_b - beside * inv_ab
-                    by_b = beside * inv_a - above * inv_ab
-                    by_a = jnp.where(first, -inv_b, jnp.where(second, inv_ab, by_a))
-                    by_b = jnp.where(first, inv_ab, jnp.where(second, -inv_a, by_b))
+                    by_a = above * bb - beside * ab
+                    by_b = beside * aa - above * ab
+                    by_a = jnp.where(first, -bb, jnp.where(second, ab, by_a))
+                    by_b = jnp.where(first, ab, jnp.where(second, -aa, by_b))
                     for k in range(r + 2, SUBLANES):
-                        column[k] = jnp.where(pivot, 0.0, column[k]) - (
-                            by_a * row_spread(column[k], r) + by_b * row_spread(column[k], r + 1)
+                        change = by_a * row_spread(column[k], r) + by_b * row_spread(
+                            column[k], r + 1
                         )
-                    rows[b] = jnp.where(pivot, 0.0, rows[b]) - (by_a * row_a + by_b * row_b)
+                        column[k] = jnp.where(pivot, 0.0, column[k]) - change * inverse
+                    change = by_a * row_a + by_b * row_b
+                    rows[b] = jnp.where(pivot, 0.0, rows[b]) - change * inverse
         for b in range(count):
             keep(b, t, done[b])
             factors[b][t] = done[b]
@@ -411,20 +436,42 @@
                     )
             elif end < block_count:
                 upper = jnp.concatenate(factors[b][panel:end], axis=0)
-                lower = jnp.transpose(upper)[SUBLANES * end :, :]
-                change = jnp.dot(
-                    lower, upper, precision=HIGHEST, preferred_element_type=jnp.float32
+                parts = split_parts(upper)
+                left = jnp.concatenate([parts[p] for p, _ in PART_PAIRS], axis=0)
+                right = jnp.concatenate([parts[p] for _, p in PART_PAIRS], axis=0)
+                change = lax.dot_general(
+                    left.astype(jnp.bfloat16),
+                    right.astype(jnp.bfloat16),
+                    (((0,), (0,)), ((), ())),
+                    preferred_element_type=jnp.float32,
                 )
                 for i in range(end, block_count):
-                    at = SUBLANES * (i - end)
-                    blocks[b][i] = blocks[b][i] - change[at : at + SUBLANES, :]
+                    blocks[b][i] = blocks[b][i] - change[SUBLANES * i : SUBLANES * (i + 1), :]
     return corner
 
 
-def factor_body(
-    gram_ref, moment_ref, held_ref, other_ref, coeffs_ref, top_factor_ref, top_coeffs_ref, *scratch, node_count
+def finish_body(
+    gram_ref,
+    moment_ref,
+    held_ref,
+    other_ref,
+    flags_ref,
+    centre_ref,
+    target_ref,
+    before_ref,
+    near_ref,
+    coeffs_ref,
+    top_factor_ref,
+    top_coeffs_ref,
+    upper_ref,
+    one_ref,
+    total_ref,
+    factor_ref,
+    charge_ref,
+    *,
+    node_count,
+    leaf_size,
 ):
-    upper_ref, one_ref = scratch
     per_device, _, rank = gram_ref.shape
     count = per_device + 1
     block_count = rank // SUBLANES
@@ -442,10 +489,31 @@
         columns = jnp.transpose(jnp.broadcast_to(moment, (rank, rank)))
         moments.append([columns[SUBLANES * i : SUBLANES * (i + 1), :] for i in range(block_count)])
 
+    group = factor_ref.shape[0]
+    leaf_rows = leaf_size // LANES * COORDS
+    points_rows = other_ref.shape[0] - fold_rows(rank)
+    centre = centre_ref[...]
+    for leaf in range(group):
+        row = points_rows - (group - leaf) * leaf_rows
+        factor, charge = source_blocks(other_ref, row, leaf_size, centre)
+        factor_ref[leaf] = factor
+        charge_ref[leaf, 0:1, :] = charge
+    total_ref[...] = before_ref[...]
+    steps = near_steps(
+        total_ref,
+        near_ref,
+        factor_ref,
+        charge_ref,
+        flags_ref,
+        target_ref,
+        flags_ref.shape[0] - group,
+        leaf_size,
+    )
+
     def keep(b, t, block):
         upper_ref[b, SUBLANES * t : SUBLANES * (t + 1), :] = block
 
-    corner = factor_all(blocks, moments, keep, one_ref[...], 8)
+    corner = factor_all(blocks, moments, keep, one_ref[...], 4, steps)
     for member in range(per_device):
         coeffs_ref[member : member + 1, :] = jnp.transpose(upper_ref[member])[0:1, :]
     lower = jnp.transpose(upper_ref[per_device])
@@ -549,7 +617,7 @@
         name="merge",
     )(payload, other_half, side)
 
-    def near(first, last, sources, final):
+    def near(first, last, sources):
         return pl.pallas_call(
             functools.partial(
                 near_body,
@@ -557,49 +625,53 @@
                 last=last,
                 leaf_size=leaf_size,
                 source_count=len(sources),
-                final=final,
             ),
-            out_shape=jax.ShapeDtypeStruct((per_device * pieces, LANES), f32) if final else totals,
+            out_shape=totals,
             in_specs=[VMEM_SPEC] * (4 + len(sources)),
             out_specs=VMEM_SPEC,
-            scratch_shapes=[pltpu.VMEM(totals.shape, f32)] if final else [],
-            input_output_aliases={} if final else {3: 0},
+            input_output_aliases={3: 0},
             compiler_params=params,
             cost_estimate=work,
-            name="near_rest" if final else "near_first",
+            name="near_part",
         )(flags, centre, target, total, *sources)
 
+    group = 3 * per_device
     arrived = []
     apart = 1
     while apart < half:
         arrived.append(across(held, apart))
         if apart == 1:
-            total = near(per_device, 3 * per_device, [held], False)
+            total = near(per_device, group, [held])
         if 2 * apart < half:
             rows = held.shape[0] - fold_rows(rank)
             held = jnp.concatenate(
                 [held[:rows], arrived[-1][:rows], held[rows:] + arrived[-1][rows:]]
             )
         apart *= 2
-    potential = near(3 * per_device, numbers, arrived, True)
+    if numbers > 2 * group:
+        total = near(group, numbers - group, arrived)
 
     share = rank // node_count
-    coeffs, top_factor, top_coeffs = pl.pallas_call(
-        functools.partial(factor_body, node_count=node_count),
+    potential, coeffs, top_factor, top_coeffs = pl.pallas_call(
+        functools.partial(finish_body, node_count=node_count, leaf_size=leaf_size),
         out_shape=(
+            jax.ShapeDtypeStruct((per_device * pieces, LANES), f32),
             jax.ShapeDtypeStruct((per_device, rank), f32),
             jax.ShapeDtypeStruct((1, share, rank), f32),
             jax.ShapeDtypeStruct((1, share), f32),
         ),
-        in_specs=[VMEM_SPEC] * 4,
-        out_specs=(VMEM_SPEC,) * 3,
+        in_specs=[VMEM_SPEC] * 8,
+        out_specs=(VMEM_SPEC,) * 4,
         scratch_shapes=[
             pltpu.VMEM((per_device + 1, rank, rank), f32),
             pltpu.VMEM((SUBLANES, rank), f32),
+            pltpu.VMEM(totals.shape, f32),
+            pltpu.VMEM((group, SUBLANES * len(PART_PAIRS), leaf_size), jnp.bfloat16),
+            pltpu.VMEM((group, SUBLANES, leaf_size), f32),
         ],
-        compiler_params=pltpu.CompilerParams(vmem_limit_bytes=VMEM_LIMIT),
-        name="factors",
-    )(gram, moment, held, arrived[-1])
+        compiler_params=params,
+        name="finish",
+    )(gram, moment, held, arrived[-1], flags, centre, target, total)
     return (potential.reshape(-1), coeffs, top_factor, top_coeffs)
 
 

time: 25.9 us -> 23.6 us (0.911)
  the two profiles are of different devices: /device:TPU:2 before, /device:TPU:4 now
where the time goes in v2:
time: 23.6 us; the launch traced here: 23.3 us
  Pallas kernels  10.5 us (44%)
  starting transfers between devices  6.56 us (28%)
  waiting for transfers between devices  5.6 us (24%)
  between operations  0.67 us (3%)
    pallas_call x1, Pallas kernels, body(): pl.pallas_call(functools.partial(finish_body, node_count=node_count, leaf...  5.28 us
    ppermute x2, starting transfers between devices, across(): lax.ppermute(block, 'node', [(z, z ^ apart) for z in range(node_count)])  4.3 us
    ppermute x1, waiting for transfers between devices, diagonal(): return lax.ppermute(block, ('leaf', 'node'), route)  3.96 us
    pallas_call x1, Pallas kernels, body(): pl.pallas_call(gram_body, out_shape=(jax.ShapeDtypeStruct((points_rows, L...  2.45 us
    ppermute x1, starting transfers between devices, diagonal(): return lax.ppermute(block, ('leaf', 'node'), route)  2.26 us
    ppermute x2, waiting for transfers between devices, across(): lax.ppermute(block, 'node', [(z, z ^ apart) for z in range(node_count)])  1.65 us
    pallas_call x1, Pallas kernels, body(): pl.pallas_call(functools.partial(own_body, node_count=node_count), out_sh...  1.51 us
    pallas_call x1, Pallas kernels, near(): pl.pallas_call(functools.partial(near_body, first=first, last=last, leaf_...  1.26 us
  transfers between devices with their start and end apart: 3, of which 2 were waited for; matrix products, arithmetic and copies ran while one was open for 0% of the time, Pallas kernels for 12%

profile of v2, /device:TPU:4, one launch (start us, length us, event | category | flops | bytes accessed | tf_op | source)
XLA Modules:
  0.0 23.3 jit_solution(6744307899511766016)
XLA Ops:
  0.6 2.5 %gram.1 = (f32[32,128]{1,0:T(8,128)S(1)}, f32[104,128]{1,0:T(8,128)S(1)}, bf16[1024,64]{1,0:T(8,128)(2,1)S(1)}, f32[8,128]{1,0:T(8,128)S(1)}, f32[2,128,128]{2,1,0:T(8,128)S(1)}, /*index=5*/f32[2,128]{1,0:T(2,128)S(1)}) custom-call(f32[3,1024]{1,0:T(4,128)} %positions_hbm.1, f32[8,128]{1,0:T(8,128)} %bitcast.3, f32[1024,128]{1,0:T(8,128)} %far_hbm.1, ...), custom_call_target="tpu_custom_call" | custom-call | tf_op jit(solution)/shard_map/gram/pallas_call | solution.py:561
  3.1 2.7 %collective-permute-start = (f32[104,128]{1,0:T(8,128)S(1)}, f32[104,128]{1,0:T(8,128)S(1)}, u32[]{:S(2)}, u32[]{:S(2)}) collective-permute-start(f32[104,128]{1,0:T(8,128)S(1)} %get-tuple-element.18.payload_ref), channel_id=1, source_target_pairs={{0,2},{1,3},{2,0},{3,1},{4,6},{5,7},{6,4},{7,5},{8,10},{9,11},{10,... | collective-permute-start | bytes 159752 | tf_op jit(solution)/shard_map/ppermute | solution.py:550
  5.7 2.3 %collective-permute-start.1 = (f32[32,128]{1,0:T(8,128)S(1)}, f32[32,128]{1,0:T(8,128)S(1)}, u32[]{:S(2)}, u32[]{:S(2)}) collective-permute-start(f32[32,128]{1,0:T(8,128)S(1)} %get-tuple-element.19), channel_id=1, source_target_pairs={{2,4},{3,5},{4,2},{5,3},{6,8},{7,9},{8,6},{9,7},{10,12},{11,13},{1... | collective-permute-start | bytes 49160 | tf_op jit(solution)/shard_map/ppermute | solution.py:559
  8.0 1.5 %near_own.1 = (f32[1024,128]{1,0:T(8,128)S(1)}, f32[12,8,128]{2,1,0:T(8,128)S(1)}) custom-call(s32[2,11]{1,0:T(2,128)} %list_hbm.1, s32[2]{0:T(128)} %count_hbm.1, f32[104,128]{1,0:T(8,128)S(1)} %get-tuple-element.18.payload_ref, bf16[1024,64]{1,0:T(8,128)(2,1)S(1)} %get-tuple-element.20.target_ref.refs_2_, f32[8,128]{1,0:T(8,128)S(1)} %get-tuple-element.21.centre_ref.refs_1_), custom_call_target="tpu_custom_call" | custom-call | flops 2147483648 | bytes 1048576 | tf_op jit(solution)/shard_map/near_own/pallas_call | solution.py:597
  9.5 4.0 %collective-permute-done.1.side_ref = f32[32,128]{1,0:T(8,128)S(1)} collective-permute-done((f32[32,128]{1,0:T(8,128)S(1)}, f32[32,128]{1,0:T(8,128)S(1)}, u32[]{:S(2)}, u32[]{:S(2)}) %collective-permute-start.1) | collective-permute-done | bytes 16416 | tf_op jit(solution)/shard_map/ppermute | solution.py:559
  13.5 0.0 collective-permute-done.other_ref
  13.5 1.6 %collective-permute-start.2 = (f32[168,128]{1,0:T(8,128)S(1)}, f32[168,128]{1,0:T(8,128)S(1)}, u32[]{:S(2)}, u32[]{:S(2)}) collective-permute-start(f32[168,128]{1,0:T(8,128)S(1)} %merge.1.refs_4_.held_ref), channel_id=1, source_target_pairs={{0,1},{1,0},{2,3},{3,2},{4,5},{5,4},{6,7},{7,6},{8,9},{9,8},{10,11... | collective-permute-start | bytes 258056 | tf_op jit(solution)/shard_map/ppermute | solution.py:550
  15.2 1.3 %near_part.1.before_ref = f32[1024,128]{1,0:T(8,128)S(1)} custom-call(f32[12,8,128]{2,1,0:T(8,128)S(1)} %get-tuple-element.22.refs_0_.flags_ref, f32[8,128]{1,0:T(8,128)S(1)} %get-tuple-element.21.centre_ref.refs_1_, bf16[1024,64]{1,0:T(8,128)(2,1)S(1)} %get-tuple-element.20.target_ref.refs_2_, ...), custom_call_target="tpu_custom_call", output_to_operand_aliasing={{}: (3, {})} | custom-call | flops 2147483648 | bytes 1048576 | tf_op jit(solution)/shard_map/near_part/pallas_call | solution.py:621
  16.4 1.6 %collective-permute-done.2.other_ref = f32[168,128]{1,0:T(8,128)S(1)} collective-permute-done((f32[168,128]{1,0:T(8,128)S(1)}, f32[168,128]{1,0:T(8,128)S(1)}, u32[]{:S(2)}, u32[]{:S(2)}) %collective-permute-start.2) | collective-permute-done | bytes 86048 | tf_op jit(solution)/shard_map/ppermute | solution.py:550
  18.1 5.3 %finish.1 = (f32[8,128]{1,0:T(8,128)}, f32[2,128]{1,0:T(2,128)}, f32[1,32,128]{2,1,0:T(8,128)}, f32[1,32]{1,0:T(1,128)}) custom-call(f32[2,128,128]{2,1,0:T(8,128)S(1)} %get-tuple-element.16.gram_ref, f32[2,128]{1,0:T(2,128)S(1)} %get-tuple-element.17.moment_ref, f32[168,128]{1,0:T(8,128)S(1)} %merge.1.refs_4_.held_ref, ...), custom_call_target="tpu_custom_call" | custom-call | tf_op jit(solution)/shard_map/finish/pallas_call | solution.py:655
  (1 shorter events, 0.0 us)
Async XLA Ops:
  3.1 10.4 %collective-permute-start = (f32[104,128]{1,0:T(8,128)S(1)}, f32[104,128]{1,0:T(8,128)S(1)}, u32[]{:S(2)}, u32[]{:S(2)}) collective-permute-start(f32[104,128]{1,0:T(8,128)S(1)} %get-tuple-element.18.payload_ref), channel_id=1, source_target_pairs={{0,2},{1,3},{2,0},{3,1},{4,6},{5,7},{6,4},{7,5},{8,10},{9,11},{10,... | collective-permute-start | bytes 159752 | tf_op jit(solution)/shard_map/ppermute | solution.py:550
  5.7 7.7 %collective-permute-start.1 = (f32[32,128]{1,0:T(8,128)S(1)}, f32[32,128]{1,0:T(8,128)S(1)}, u32[]{:S(2)}, u32[]{:S(2)}) collective-permute-start(f32[32,128]{1,0:T(8,128)S(1)} %get-tuple-element.19), channel_id=1, source_target_pairs={{2,4},{3,5},{4,2},{5,3},{6,8},{7,9},{8,6},{9,7},{10,12},{11,13},{1... | collective-permute-start | bytes 49160 | tf_op jit(solution)/shard_map/ppermute | solution.py:559
  13.5 4.6 %collective-permute-start.2 = (f32[168,128]{1,0:T(8,128)S(1)}, f32[168,128]{1,0:T(8,128)S(1)}, u32[]{:S(2)}, u32[]{:S(2)}) collective-permute-start(f32[168,128]{1,0:T(8,128)S(1)} %merge.1.refs_4_.held_ref), channel_id=1, source_target_pairs={{0,1},{1,0},{2,3},{3,2},{4,5},{5,4},{6,7},{7,6},{8,9},{9,8},{10,11... | collective-permute-start | bytes 258056 | tf_op jit(solution)/shard_map/ppermute | solution.py:550

commit v3 on v2

--- a/solution.py
+++ b/solution.py
@@ -98,19 +98,15 @@
 
 
 def gram_body(
-    positions_hbm,
-    charges_hbm,
+    points_ref,
     far_hbm,
     proxies_hbm,
     strengths_hbm,
-    points_ref,
-    payload_ref,
+    total_ref,
     target_ref,
     centre_ref,
     gram_ref,
     moment_ref,
-    positions_ref,
-    charges_ref,
     far_ref,
     proxies_ref,
     strengths_ref,
@@ -119,12 +115,7 @@
     per_device, rank = strengths_ref.shape
     leaf_size = far_ref.shape[0] // per_device
     pieces = leaf_size // LANES
-    pairs = [
-        (positions_hbm, positions_ref),
-        (charges_hbm, charges_ref),
-        (proxies_hbm, proxies_ref),
-        (strengths_hbm, strengths_ref),
-    ]
+    pairs = [(proxies_hbm, proxies_ref), (strengths_hbm, strengths_ref)]
     for member in range(per_device):
         span = slice(member * leaf_size, (member + 1) * leaf_size)
         pairs.append((far_hbm.at[span], far_ref.at[span]))
@@ -134,35 +125,40 @@
     ]
     for copy in copies:
         copy.start()
-    for copy in copies[:4]:
-        copy.wait()
-
-    points = padded_rows(positions_ref[...])
+
+    blocks = [
+        points_ref[at * COORDS : (at + 1) * COORDS, :] for at in range(per_device * pieces)
+    ]
     centre = jnp.zeros((SUBLANES, 1), jnp.float32)
     for member in range(per_device):
-        centre = centre + (jnp.floor(points[:, member * leaf_size : member * leaf_size + 1]) + 0.5)
+        centre = centre + (jnp.floor(padded_rows(blocks[member * pieces][:, 0:1])) + 0.5)
     centre = jnp.where(row_of(centre.shape) < 3, centre / per_device, 0.0)
     centre_ref[...] = jnp.broadcast_to(centre, centre_ref.shape)
-    shifted = points - centre
+    targets = []
+    for member in range(per_device):
+        span = slice(member * leaf_size, (member + 1) * leaf_size)
+        shifted = jnp.concatenate(
+            [
+                padded_rows(block) - centre
+                for block in blocks[member * pieces : (member + 1) * pieces]
+            ],
+            axis=1,
+        )
+        targets.append(jnp.transpose(target_factor(shifted)).astype(jnp.bfloat16))
+        target_ref[span, :] = targets[-1]
+    for copy in copies[:2]:
+        copy.wait()
     total_gram = jnp.zeros((rank, rank), jnp.float32)
     total_moment = jnp.zeros((1, rank), jnp.float32)
     for member in range(per_device):
         span = slice(member * leaf_size, (member + 1) * leaf_size)
-        for piece in range(pieces):
-            at = (member * pieces + piece) * COORDS
-            lanes = slice(span.start + piece * LANES, span.start + (piece + 1) * LANES)
-            points_ref[at : at + 3, :] = positions_ref[:, lanes]
-            points_ref[at + 3 : at + 4, :] = charges_ref[at // COORDS : at // COORDS + 1, :]
-        target = jnp.transpose(target_factor(shifted[:, span])).astype(jnp.bfloat16)
-        target_ref[span, :] = target
         proxies = jnp.concatenate([proxies_ref[c, member : member + 1, :] for c in range(3)], axis=0)
         source = source_factor(padded_rows(proxies) - centre)
-        kernel_values = lax.rsqrt(squares(target, source))
-        copies[4 + member].wait()
+        kernel_values = lax.rsqrt(squares(targets[member], source))
+        copies[2 + member].wait()
         response = far_ref[span, :] + kernel_values * strengths_ref[member : member + 1, :]
         weights = jnp.concatenate(
-            [charges_ref[member * pieces + p : member * pieces + p + 1, :] for p in range(pieces)],
-            axis=1,
+            [block[3:4, :] for block in blocks[member * pieces : (member + 1) * pieces]], axis=1
         )
         left = jnp.concatenate(
             [jnp.transpose(response), jnp.broadcast_to(weights, (SUBLANES, leaf_size))], axis=0
@@ -172,9 +168,7 @@
         moment_ref[member : member + 1, :] = both[rank : rank + 1, :]
         total_gram = total_gram + both[:rank, :]
         total_moment = total_moment + both[rank : rank + 1, :]
-    points_rows = per_device * pieces * COORDS
-    payload_ref[:points_rows, :] = points_ref[...]
-    payload_ref[points_rows:, :] = fold(total_gram, total_moment)
+    total_ref[...] = fold(total_gram, total_moment)
 
 
 def lane_sums(block):
@@ -218,7 +212,7 @@
 def own_body(
     list_hbm,
     count_hbm,
-    payload_ref,
+    points_ref,
     target_ref,
     centre_ref,
     total_ref,
@@ -241,7 +235,7 @@
         copy.start()
     centre = centre_ref[...]
     items = [
-        source_blocks(payload_ref, leaf * leaf_rows, leaf_size, centre)
+        source_blocks(points_ref, leaf * leaf_rows, leaf_size, centre)
         for leaf in range(per_device)
     ]
     for copy in copies:
@@ -275,11 +269,18 @@
     add_sources(total_ref, None, target_ref, items, flags, per_device, leaf_size)
 
 
-def merge_body(payload_ref, other_ref, side_ref, held_ref, *, rows):
-    held_ref[0:rows, :] = payload_ref[0:rows, :]
-    held_ref[rows : 2 * rows, :] = other_ref[0:rows, :]
-    held_ref[2 * rows : 3 * rows, :] = side_ref[0:rows, :]
-    held_ref[3 * rows :, :] = payload_ref[rows:, :] + other_ref[rows:, :]
+def payload_body(points_ref, side_ref, total_ref, payload_ref):
+    rows = points_ref.shape[0]
+    payload_ref[0:rows, :] = points_ref[...]
+    payload_ref[rows : 2 * rows, :] = side_ref[...]
+    payload_ref[2 * rows :, :] = total_ref[...]
+
+
+def merge_body(points_ref, total_ref, other_ref, held_ref):
+    rows = points_ref.shape[0]
+    held_ref[0:rows, :] = points_ref[...]
+    held_ref[rows : 3 * rows, :] = other_ref[0 : 2 * rows, :]
+    held_ref[3 * rows :, :] = total_ref[...] + other_ref[2 * rows :, :]
 
 
 def near_body(*refs, first, last, leaf_size, source_count):
@@ -549,51 +550,54 @@
     def across(block, apart):
         return lax.ppermute(block, "node", [(z, z ^ apart) for z in range(node_count)])
 
-    def diagonal(block):
+    def sideways(block):
         route = []
         for at in range(block_total):
             for z in range(node_count):
                 to = at + 1 if z >= half else at - 1
                 if 0 <= to < block_total:
-                    route.append((at * node_count + z, to * node_count + (z ^ half)))
+                    route.append((at * node_count + z, to * node_count + z))
         return lax.ppermute(block, ("leaf", "node"), route)
 
-    points, payload, target, centre, gram, moment = pl.pallas_call(
+    params = pltpu.CompilerParams(vmem_limit_bytes=VMEM_LIMIT)
+    work = pl.CostEstimate(flops=1 << 31, bytes_accessed=1 << 20, transcendentals=0)
+    points = jnp.concatenate([positions, charges[None, :]], 0)
+    points = points.reshape(COORDS, per_device * pieces, LANES).transpose(1, 0, 2)
+    points = points.reshape(points_rows, LANES)
+    side = sideways(points)
+    total_gram, target, centre, gram, moment = pl.pallas_call(
         gram_body,
         out_shape=(
-            jax.ShapeDtypeStruct((points_rows, LANES), f32),
-            jax.ShapeDtypeStruct((points_rows + fold_rows(rank), rank), f32),
+            jax.ShapeDtypeStruct((fold_rows(rank), rank), f32),
             jax.ShapeDtypeStruct((per_device * leaf_size, SUBLANES * len(PART_PAIRS)), jnp.bfloat16),
             jax.ShapeDtypeStruct((SUBLANES, LANES), f32),
             jax.ShapeDtypeStruct((per_device, rank, rank), f32),
             jax.ShapeDtypeStruct((per_device, rank), f32),
         ),
-        in_specs=[HBM_SPEC] * 5,
-        out_specs=(VMEM_SPEC,) * 6,
+        in_specs=[VMEM_SPEC] + [HBM_SPEC] * 3,
+        out_specs=(VMEM_SPEC,) * 5,
         scratch_shapes=[
-            pltpu.VMEM(positions.shape, f32),
-            pltpu.VMEM((per_device * pieces, LANES), f32),
             pltpu.VMEM(far_sample.shape, f32),
             pltpu.VMEM((3, per_device, rank), f32),
             pltpu.VMEM(strengths.shape, f32),
-            pltpu.SemaphoreType.DMA((4 + per_device,)),
+            pltpu.SemaphoreType.DMA((2 + per_device,)),
         ],
-        compiler_params=pltpu.CompilerParams(vmem_limit_bytes=VMEM_LIMIT),
+        compiler_params=params,
+        cost_estimate=work,
         name="gram",
-    )(
-        in_hbm(positions),
-        in_hbm(charges.reshape(per_device * pieces, LANES)),
-        in_hbm(far_sample),
-        in_hbm(proxies.transpose(1, 0, 2)),
-        in_hbm(strengths),
-    )
+    )(points, in_hbm(far_sample), in_hbm(proxies.transpose(1, 0, 2)), in_hbm(strengths))
 
     totals = jax.ShapeDtypeStruct((per_device * leaf_size, LANES), f32)
     numbers = 3 * half * per_device
-    params = pltpu.CompilerParams(vmem_limit_bytes=VMEM_LIMIT)
-    work = pl.CostEstimate(flops=1 << 31, bytes_accessed=1 << 20, transcendentals=0)
+    payload = pl.pallas_call(
+        payload_body,
+        out_shape=jax.ShapeDtypeStruct((2 * points_rows + fold_rows(rank), rank), f32),
+        in_specs=[VMEM_SPEC] * 3,
+        out_specs=VMEM_SPEC,
+        compiler_params=params,
+        name="payload",
+    )(points, side, total_gram)
     other_half = across(payload, half)
-    side = diagonal(points)
     total, flags = pl.pallas_call(
         functools.partial(own_body, node_count=node_count),
         out_shape=(totals, jax.ShapeDtypeStruct((numbers, SUBLANES, LANES), f32)),
@@ -607,15 +611,15 @@
         compiler_params=params,
         cost_estimate=work,
         name="near_own",
-    )(in_hbm(near_list), in_hbm(near_count), payload, target, centre)
+    )(in_hbm(near_list), in_hbm(near_count), points, target, centre)
     held = pl.pallas_call(
-        functools.partial(merge_body, rows=points_rows),
+        merge_body,
         out_shape=jax.ShapeDtypeStruct((3 * points_rows + fold_rows(rank), rank), f32),
         in_specs=[VMEM_SPEC] * 3,
         out_specs=VMEM_SPEC,
         compiler_params=params,
         name="merge",
-    )(payload, other_half, side)
+    )(points, total_gram, other_half)
 
     def near(first, last, sources):
         return pl.pallas_call(

time: 23.6 us -> 24 us (1.017)
  the two profiles are of different devices: /device:TPU:4 before, /device:TPU:0 now
where the time goes in v3:
time: 24 us; the launch traced here: 23.6 us
  Pallas kernels  10.4 us (43%)
  starting transfers between devices  9.07 us (38%)
  waiting for transfers between devices  2.69 us (11%)
  other arithmetic  0.75 us (3%)
  between operations  0.68 us (3%)
    ppermute x2, starting transfers between devices, across(): lax.ppermute(block, 'node', [(z, z ^ apart) for z in range(node_count)])  7.78 us
    pallas_call x1, Pallas kernels, body(): pl.pallas_call(functools.partial(finish_body, node_count=node_count, leaf...  5.26 us
    ppermute x2, waiting for transfers between devices, across(): lax.ppermute(block, 'node', [(z, z ^ apart) for z in range(node_count)])  2.69 us
    pallas_call x1, Pallas kernels, body(): pl.pallas_call(gram_body, out_shape=(jax.ShapeDtypeStruct((fold_rows(rank...  2.4 us
    pallas_call x1, Pallas kernels, body(): pl.pallas_call(functools.partial(own_body, node_count=node_count), out_sh...  1.5 us
    ppermute x1, starting transfers between devices, sideways(): return lax.ppermute(block, ('leaf', 'node'), route)  1.29 us
    pallas_call x1, Pallas kernels, near(): pl.pallas_call(functools.partial(near_body, first=first, last=last, leaf_...  1.26 us
    concatenate x1, other arithmetic, body(): points = jnp.concatenate([positions, charges[None, :]], 0)  0.75 us
  transfers between devices with their start and end apart: 3, of which 2 were waited for; matrix products, arithmetic and copies ran while one was open for 0% of the time, Pallas kernels for 22%

profile of v3, /device:TPU:0, one launch (start us, length us, event | category | flops | bytes accessed | tf_op | source)
XLA Modules:
  0.0 23.6 jit_solution(6775180599965537126)
XLA Ops:
  0.6 0.7 %pad_maximum_fusion = f32[4,8,128]{2,0,1:T(4,128)S(1)} fusion(f32[1,8,128]{2,0,1:T(1,128)} %bitcast.13, f32[3,8,128]{2,0,1:T(4,128)} %bitcast.12), kind=kLoop, calls=%fused_computation | loop fusion | flops 4096 | bytes 32768 | tf_op jit(solution)/shard_map/concatenate | solution.py:564
  1.4 1.3 %collective-permute-start = (f32[32,128]{1,0:T(8,128)S(1)}, f32[32,128]{1,0:T(8,128)S(1)}, u32[]{:S(2)}, u32[]{:S(2)}) collective-permute-start(f32[32,128]{1,0:T(8,128)S(1)} %bitcast.7), channel_id=1, source_target_pairs={{2,6},{3,7},{4,0},{5,1},{6,10},{7,11},{8,4},{9,5},{10,14},{11,15},... | collective-permute-start | bytes 49160 | tf_op jit(solution)/shard_map/ppermute | solution.py:560
  2.7 2.4 %gram.1 = (f32[72,128]{1,0:T(8,128)S(1)}, bf16[1024,64]{1,0:T(8,128)(2,1)S(1)}, f32[8,128]{1,0:T(8,128)S(1)}, f32[2,128,128]{2,1,0:T(8,128)S(1)}, f32[2,128]{1,0:T(2,128)S(1)}) custom-call(f32[32,128]{1,0:T(8,128)S(1)} %bitcast.8, f32[1024,128]{1,0:T(8,128)} %far_hbm.1, f32[3,2,128]{2,1,0:T(2,128)} %bitcast.15, f32[2,128]{1,0:T(2,128)} %strengths_hbm.1), custom_call_target="tpu_custom_call" | custom-call | flops 2147483648 | bytes 1048576 | tf_op jit(solution)/shard_map/gram/pallas_call | solution.py:568
  5.1 0.0 collective-permute-done.side_ref
  5.1 4.5 %collective-permute-start.1 = (f32[136,128]{1,0:T(8,128)S(1)}, f32[136,128]{1,0:T(8,128)S(1)}, u32[]{:S(2)}, u32[]{:S(2)}) collective-permute-start(f32[136,128]{1,0:T(8,128)S(1)} %payload.1), channel_id=1, source_target_pairs={{0,2},{1,3},{2,0},{3,1},{4,6},{5,7},{6,4},{7,5},{8,10},{9,11},{10,... | collective-permute-start | bytes 208904 | tf_op jit(solution)/shard_map/ppermute | solution.py:551
  9.7 1.5 %near_own.1 = (f32[1024,128]{1,0:T(8,128)S(1)}, f32[12,8,128]{2,1,0:T(8,128)S(1)}) custom-call(s32[2,11]{1,0:T(2,128)} %list_hbm.1, s32[2]{0:T(128)} %count_hbm.1, f32[32,128]{1,0:T(8,128)S(1)} %bitcast.10, bf16[1024,64]{1,0:T(8,128)(2,1)S(1)} %get-tuple-element.18.target_ref.refs_2_, f32[8,128]{1,0:T(8,128)S(1)} %get-tuple-element.19.centre_ref.refs_1_), custom_call_target="tpu_custom_call" | custom-call | flops 2147483648 | bytes 1048576 | tf_op jit(solution)/shard_map/near_own/pallas_call | solution.py:601
  11.2 0.8 %collective-permute-done.1.other_ref = f32[136,128]{1,0:T(8,128)S(1)} collective-permute-done((f32[136,128]{1,0:T(8,128)S(1)}, f32[136,128]{1,0:T(8,128)S(1)}, u32[]{:S(2)}, u32[]{:S(2)}) %collective-permute-start.1) | collective-permute-done | bytes 69664 | tf_op jit(solution)/shard_map/ppermute | solution.py:551
  12.0 3.2 %collective-permute-start.2 = (f32[168,128]{1,0:T(8,128)S(1)}, f32[168,128]{1,0:T(8,128)S(1)}, u32[]{:S(2)}, u32[]{:S(2)}) collective-permute-start(f32[168,128]{1,0:T(8,128)S(1)} %merge.1.refs_4_.held_ref), channel_id=1, source_target_pairs={{0,1},{1,0},{2,3},{3,2},{4,5},{5,4},{6,7},{7,6},{8,9},{9,8},{10,11... | collective-permute-start | bytes 258056 | tf_op jit(solution)/shard_map/ppermute | solution.py:551
  15.2 1.3 %near_part.1.before_ref = f32[1024,128]{1,0:T(8,128)S(1)} custom-call(f32[12,8,128]{2,1,0:T(8,128)S(1)} %get-tuple-element.20.refs_0_.flags_ref, f32[8,128]{1,0:T(8,128)S(1)} %get-tuple-element.19.centre_ref.refs_1_, bf16[1024,64]{1,0:T(8,128)(2,1)S(1)} %get-tuple-element.18.target_ref.refs_2_, ...), custom_call_target="tpu_custom_call", output_to_operand_aliasing={{}: (3, {})} | custom-call | flops 2147483648 | bytes 1048576 | tf_op jit(solution)/shard_map/near_part/pallas_call | solution.py:625
  16.5 1.9 %collective-permute-done.2.other_ref = f32[168,128]{1,0:T(8,128)S(1)} collective-permute-done((f32[168,128]{1,0:T(8,128)S(1)}, f32[168,128]{1,0:T(8,128)S(1)}, u32[]{:S(2)}, u32[]{:S(2)}) %collective-permute-start.2) | collective-permute-done | bytes 86048 | tf_op jit(solution)/shard_map/ppermute | solution.py:551
  18.4 5.3 %finish.1 = (f32[8,128]{1,0:T(8,128)}, f32[2,128]{1,0:T(2,128)}, f32[1,32,128]{2,1,0:T(8,128)}, f32[1,32]{1,0:T(1,128)}) custom-call(f32[2,128,128]{2,1,0:T(8,128)S(1)} %get-tuple-element.15.gram_ref, f32[2,128]{1,0:T(2,128)S(1)} %get-tuple-element.16.moment_ref, f32[168,128]{1,0:T(8,128)S(1)} %merge.1.refs_4_.held_ref, ...), custom_call_target="tpu_custom_call" | custom-call | tf_op jit(solution)/shard_map/finish/pallas_call | solution.py:659
  (2 shorter events, 0.0 us)
Async XLA Ops:
  1.4 3.7 %collective-permute-start = (f32[32,128]{1,0:T(8,128)S(1)}, f32[32,128]{1,0:T(8,128)S(1)}, u32[]{:S(2)}, u32[]{:S(2)}) collective-permute-start(f32[32,128]{1,0:T(8,128)S(1)} %bitcast.7), channel_id=1, source_target_pairs={{2,6},{3,7},{4,0},{5,1},{6,10},{7,11},{8,4},{9,5},{10,14},{11,15},... | collective-permute-start | bytes 49160 | tf_op jit(solution)/shard_map/ppermute | solution.py:560
  5.1 6.8 %collective-permute-start.1 = (f32[136,128]{1,0:T(8,128)S(1)}, f32[136,128]{1,0:T(8,128)S(1)}, u32[]{:S(2)}, u32[]{:S(2)}) collective-permute-start(f32[136,128]{1,0:T(8,128)S(1)} %payload.1), channel_id=1, source_target_pairs={{0,2},{1,3},{2,0},{3,1},{4,6},{5,7},{6,4},{7,5},{8,10},{9,11},{10,... | collective-permute-start | bytes 208904 | tf_op jit(solution)/shard_map/ppermute | solution.py:551
  12.0 6.4 %collective-permute-start.2 = (f32[168,128]{1,0:T(8,128)S(1)}, f32[168,128]{1,0:T(8,128)S(1)}, u32[]{:S(2)}, u32[]{:S(2)}) collective-permute-start(f32[168,128]{1,0:T(8,128)S(1)} %merge.1.refs_4_.held_ref), channel_id=1, source_target_pairs={{0,1},{1,0},{2,3},{3,2},{4,5},{5,4},{6,7},{7,6},{8,9},{9,8},{10,11... | collective-permute-start | bytes 258056 | tf_op jit(solution)/shard_map/ppermute | solution.py:551

commit v4 on v3

--- a/solution.py
+++ b/solution.py
@@ -247,7 +247,7 @@
     used = jnp.zeros((per_device, slots), jnp.int32)
     for member in range(per_device):
         used = jnp.where(row == member, count_ref[member], used)
-    listed = jnp.where(slot < used, list_ref[...], -1)
+    listed = jnp.where(slot < used, list_ref[...], -(1 << 24))
     beside = jnp.where(node_index >= half, block_index + 1, block_index - 1)
     flags = []
     for number in range(flags_ref.shape[0]):
@@ -554,9 +554,8 @@
         route = []
         for at in range(block_total):
             for z in range(node_count):
-                to = at + 1 if z >= half else at - 1
-                if 0 <= to < block_total:
-                    route.append((at * node_count + z, to * node_count + z))
+                to = (at + 1 if z >= half else at - 1) % block_total
+                route.append((at * node_count + z, to * node_count + z))
         return lax.ppermute(block, ("leaf", "node"), route)
 
     params = pltpu.CompilerParams(vmem_limit_bytes=VMEM_LIMIT)

time: 24 us -> 23.8 us (level)
  starting transfers between devices: 9.07 us -> 6.26 us
  waiting for transfers between devices: 2.69 us -> 5.37 us
    ppermute x2, starting transfers between devices: 7.78 us -> 2.88 us  [across(): lax.ppermute(block, 'node', [(z, z ^ apart) for z in range(node_count)])]
    ppermute x2, waiting for transfers between devices: 2.69 us -> 5.37 us  [across(): lax.ppermute(block, 'node', [(z, z ^ apart) for z in range(node_count)])]
    ppermute x1, starting transfers between devices: 1.29 us -> 3.39 us  [sideways(): return lax.ppermute(block, ('leaf', 'node'), route)]
where the time goes in v4:
time: 23.8 us; the launch traced here: 23.5 us
  Pallas kernels  10.4 us (44%)
  starting transfers between devices  6.26 us (26%)
  waiting for transfers between devices  5.37 us (23%)
  other arithmetic  0.75 us (3%)
  between operations  0.68 us (3%)
    ppermute x2, waiting for transfers between devices, across(): lax.ppermute(block, 'node', [(z, z ^ apart) for z in range(node_count)])  5.37 us
    pallas_call x1, Pallas kernels, body(): pl.pallas_call(functools.partial(finish_body, node_count=node_count, leaf...  5.26 us
    ppermute x1, starting transfers between devices, sideways(): return lax.ppermute(block, ('leaf', 'node'), route)  3.39 us
    ppermute x2, starting transfers between devices, across(): lax.ppermute(block, 'node', [(z, z ^ apart) for z in range(node_count)])  2.88 us
    pallas_call x1, Pallas kernels, body(): pl.pallas_call(gram_body, out_shape=(jax.ShapeDtypeStruct((fold_rows(rank...  2.4 us
    pallas_call x1, Pallas kernels, body(): pl.pallas_call(functools.partial(own_body, node_count=node_count), out_sh...  1.51 us
    pallas_call x1, Pallas kernels, near(): pl.pallas_call(functools.partial(near_body, first=first, last=last, leaf_...  1.26 us
    concatenate x1, other arithmetic, body(): points = jnp.concatenate([positions, charges[None, :]], 0)  0.75 us
  transfers between devices with their start and end apart: 3, of which 2 were waited for; matrix products, arithmetic and copies ran while one was open for 0% of the time, Pallas kernels for 22%

profile of v4, /device:TPU:0, one launch (start us, length us, event | category | flops | bytes accessed | tf_op | source)
XLA Modules:
  0.0 23.5 jit_solution(16774514287251393552)
XLA Ops:
  0.6 0.7 %pad_maximum_fusion = f32[4,8,128]{2,0,1:T(4,128)S(1)} fusion(f32[1,8,128]{2,0,1:T(1,128)} %bitcast.13, f32[3,8,128]{2,0,1:T(4,128)} %bitcast.12), kind=kLoop, calls=%fused_computation | loop fusion | flops 4096 | bytes 32768 | tf_op jit(solution)/shard_map/concatenate | solution.py:563
  1.4 3.4 %collective-permute-start = (f32[32,128]{1,0:T(8,128)S(1)}, f32[32,128]{1,0:T(8,128)S(1)}, u32[]{:S(2)}, u32[]{:S(2)}) collective-permute-start(f32[32,128]{1,0:T(8,128)S(1)} %bitcast.7), channel_id=1, source_target_pairs={{0,28},{1,29},{2,6},{3,7},{4,0},{5,1},{6,10},{7,11},{8,4},{9,5},{1... | collective-permute-start | bytes 49160 | tf_op jit(solution)/shard_map/ppermute | solution.py:559
  4.8 2.4 %gram.1 = (f32[72,128]{1,0:T(8,128)S(1)}, bf16[1024,64]{1,0:T(8,128)(2,1)S(1)}, f32[8,128]{1,0:T(8,128)S(1)}, f32[2,128,128]{2,1,0:T(8,128)S(1)}, f32[2,128]{1,0:T(2,128)S(1)}) custom-call(f32[32,128]{1,0:T(8,128)S(1)} %bitcast.8, f32[1024,128]{1,0:T(8,128)} %far_hbm.1, f32[3,2,128]{2,1,0:T(2,128)} %bitcast.15, f32[2,128]{1,0:T(2,128)} %strengths_hbm.1), custom_call_target="tpu_custom_call" | custom-call | flops 2147483648 | bytes 1048576 | tf_op jit(solution)/shard_map/gram/pallas_call | solution.py:567
  7.2 0.0 collective-permute-done.side_ref
  7.2 2.3 %collective-permute-start.1 = (f32[136,128]{1,0:T(8,128)S(1)}, f32[136,128]{1,0:T(8,128)S(1)}, u32[]{:S(2)}, u32[]{:S(2)}) collective-permute-start(f32[136,128]{1,0:T(8,128)S(1)} %payload.1), channel_id=1, source_target_pairs={{0,2},{1,3},{2,0},{3,1},{4,6},{5,7},{6,4},{7,5},{8,10},{9,11},{10,... | collective-permute-start | bytes 208904 | tf_op jit(solution)/shard_map/ppermute | solution.py:551
  9.5 1.5 %near_own.1 = (f32[1024,128]{1,0:T(8,128)S(1)}, f32[12,8,128]{2,1,0:T(8,128)S(1)}) custom-call(s32[2,11]{1,0:T(2,128)} %list_hbm.1, s32[2]{0:T(128)} %count_hbm.1, f32[32,128]{1,0:T(8,128)S(1)} %bitcast.10, bf16[1024,64]{1,0:T(8,128)(2,1)S(1)} %get-tuple-element.18.target_ref.refs_2_, f32[8,128]{1,0:T(8,128)S(1)} %get-tuple-element.19.centre_ref.refs_1_), custom_call_target="tpu_custom_call" | custom-call | flops 2147483648 | bytes 1048576 | tf_op jit(solution)/shard_map/near_own/pallas_call | solution.py:600
  11.1 2.6 %collective-permute-done.1.other_ref = f32[136,128]{1,0:T(8,128)S(1)} collective-permute-done((f32[136,128]{1,0:T(8,128)S(1)}, f32[136,128]{1,0:T(8,128)S(1)}, u32[]{:S(2)}, u32[]{:S(2)}) %collective-permute-start.1) | collective-permute-done | bytes 69664 | tf_op jit(solution)/shard_map/ppermute | solution.py:551
  13.7 0.5 %collective-permute-start.2 = (f32[168,128]{1,0:T(8,128)S(1)}, f32[168,128]{1,0:T(8,128)S(1)}, u32[]{:S(2)}, u32[]{:S(2)}) collective-permute-start(f32[168,128]{1,0:T(8,128)S(1)} %merge.1.refs_4_.held_ref), channel_id=1, source_target_pairs={{0,1},{1,0},{2,3},{3,2},{4,5},{5,4},{6,7},{7,6},{8,9},{9,8},{10,11... | collective-permute-start | bytes 258056 | tf_op jit(solution)/shard_map/ppermute | solution.py:551
  14.2 1.3 %near_part.1.before_ref = f32[1024,128]{1,0:T(8,128)S(1)} custom-call(f32[12,8,128]{2,1,0:T(8,128)S(1)} %get-tuple-element.20.refs_0_.flags_ref, f32[8,128]{1,0:T(8,128)S(1)} %get-tuple-element.19.centre_ref.refs_1_, bf16[1024,64]{1,0:T(8,128)(2,1)S(1)} %get-tuple-element.18.target_ref.refs_2_, ...), custom_call_target="tpu_custom_call", output_to_operand_aliasing={{}: (3, {})} | custom-call | flops 2147483648 | bytes 1048576 | tf_op jit(solution)/shard_map/near_part/pallas_call | solution.py:624
  15.5 2.7 %collective-permute-done.2.other_ref = f32[168,128]{1,0:T(8,128)S(1)} collective-permute-done((f32[168,128]{1,0:T(8,128)S(1)}, f32[168,128]{1,0:T(8,128)S(1)}, u32[]{:S(2)}, u32[]{:S(2)}) %collective-permute-start.2) | collective-permute-done | bytes 86048 | tf_op jit(solution)/shard_map/ppermute | solution.py:551
  18.2 5.3 %finish.1 = (f32[8,128]{1,0:T(8,128)}, f32[2,128]{1,0:T(2,128)}, f32[1,32,128]{2,1,0:T(8,128)}, f32[1,32]{1,0:T(1,128)}) custom-call(f32[2,128,128]{2,1,0:T(8,128)S(1)} %get-tuple-element.15.gram_ref, f32[2,128]{1,0:T(2,128)S(1)} %get-tuple-element.16.moment_ref, f32[168,128]{1,0:T(8,128)S(1)} %merge.1.refs_4_.held_ref, ...), custom_call_target="tpu_custom_call" | custom-call | tf_op jit(solution)/shard_map/finish/pallas_call | solution.py:658
  (2 shorter events, 0.0 us)
Async XLA Ops:
  1.4 5.8 %collective-permute-start = (f32[32,128]{1,0:T(8,128)S(1)}, f32[32,128]{1,0:T(8,128)S(1)}, u32[]{:S(2)}, u32[]{:S(2)}) collective-permute-start(f32[32,128]{1,0:T(8,128)S(1)} %bitcast.7), channel_id=1, source_target_pairs={{0,28},{1,29},{2,6},{3,7},{4,0},{5,1},{6,10},{7,11},{8,4},{9,5},{1... | collective-permute-start | bytes 49160 | tf_op jit(solution)/shard_map/ppermute | solution.py:559
  7.2 6.5 %collective-permute-start.1 = (f32[136,128]{1,0:T(8,128)S(1)}, f32[136,128]{1,0:T(8,128)S(1)}, u32[]{:S(2)}, u32[]{:S(2)}) collective-permute-start(f32[136,128]{1,0:T(8,128)S(1)} %payload.1), channel_id=1, source_target_pairs={{0,2},{1,3},{2,0},{3,1},{4,6},{5,7},{6,4},{7,5},{8,10},{9,11},{10,... | collective-permute-start | bytes 208904 | tf_op jit(solution)/shard_map/ppermute | solution.py:551
  13.7 4.6 %collective-permute-start.2 = (f32[168,128]{1,0:T(8,128)S(1)}, f32[168,128]{1,0:T(8,128)S(1)}, u32[]{:S(2)}, u32[]{:S(2)}) collective-permute-start(f32[168,128]{1,0:T(8,128)S(1)} %merge.1.refs_4_.held_ref), channel_id=1, source_target_pairs={{0,1},{1,0},{2,3},{3,2},{4,5},{5,4},{6,7},{7,6},{8,9},{9,8},{10,11... | collective-permute-start | bytes 258056 | tf_op jit(solution)/shard_map/ppermute | solution.py:551

commit v5 on v2

--- a/solution.py
+++ b/solution.py
@@ -253,7 +253,7 @@
     used = jnp.zeros((per_device, slots), jnp.int32)
     for member in range(per_device):
         used = jnp.where(row == member, count_ref[member], used)
-    listed = jnp.where(slot < used, list_ref[...], -1)
+    listed = jnp.where(slot < used, list_ref[...], -(1 << 24))
     beside = jnp.where(node_index >= half, block_index + 1, block_index - 1)
     flags = []
     for number in range(flags_ref.shape[0]):
@@ -553,9 +553,8 @@
         route = []
         for at in range(block_total):
             for z in range(node_count):
-                to = at + 1 if z >= half else at - 1
-                if 0 <= to < block_total:
-                    route.append((at * node_count + z, to * node_count + (z ^ half)))
+                to = (at + 1 if z >= half else at - 1) % block_total
+                route.append((at * node_count + z, to * node_count + (z ^ half)))
         return lax.ppermute(block, ("leaf", "node"), route)
 
     points, payload, target, centre, gram, moment = pl.pallas_call(

time: 23.6 us -> 23.2 us (0.983)
  the two profiles are of different devices: /device:TPU:4 before, /device:TPU:0 now
where the time goes in v5:
time: 23.2 us; the launch traced here: 22.9 us
  Pallas kernels  10.5 us (45%)
  starting transfers between devices  7.14 us (31%)
  waiting for transfers between devices  4.59 us (20%)
  between operations  0.66 us (3%)
    ppermute x2, starting transfers between devices, across(): lax.ppermute(block, 'node', [(z, z ^ apart) for z in range(node_count)])  5.74 us
    pallas_call x1, Pallas kernels, body(): pl.pallas_call(functools.partial(finish_body, node_count=node_count, leaf...  5.26 us
    ppermute x1, waiting for transfers between devices, diagonal(): return lax.ppermute(block, ('leaf', 'node'), route)  2.94 us
    pallas_call x1, Pallas kernels, body(): pl.pallas_call(gram_body, out_shape=(jax.ShapeDtypeStruct((points_rows, L...  2.45 us
    ppermute x2, waiting for transfers between devices, across(): lax.ppermute(block, 'node', [(z, z ^ apart) for z in range(node_count)])  1.65 us
    pallas_call x1, Pallas kernels, body(): pl.pallas_call(functools.partial(own_body, node_count=node_count), out_sh...  1.51 us
    ppermute x1, starting transfers between devices, diagonal(): return lax.ppermute(block, ('leaf', 'node'), route)  1.4 us
    pallas_call x1, Pallas kernels, near(): pl.pallas_call(functools.partial(near_body, first=first, last=last, leaf_...  1.26 us
  transfers between devices with their start and end apart: 3, of which 2 were waited for; matrix products, arithmetic and copies ran while one was open for 0% of the time, Pallas kernels for 12%

profile of v5, /device:TPU:0, one launch (start us, length us, event | category | flops | bytes accessed | tf_op | source)
XLA Modules:
  0.0 22.9 jit_solution(4880731397607713773)
XLA Ops:
  0.6 2.5 %gram.1 = (f32[32,128]{1,0:T(8,128)S(1)}, f32[104,128]{1,0:T(8,128)S(1)}, bf16[1024,64]{1,0:T(8,128)(2,1)S(1)}, f32[8,128]{1,0:T(8,128)S(1)}, f32[2,128,128]{2,1,0:T(8,128)S(1)}, /*index=5*/f32[2,128]{1,0:T(2,128)S(1)}) custom-call(f32[3,1024]{1,0:T(4,128)} %positions_hbm.1, f32[8,128]{1,0:T(8,128)} %bitcast.3, f32[1024,128]{1,0:T(8,128)} %far_hbm.1, ...), custom_call_target="tpu_custom_call" | custom-call | tf_op jit(solution)/shard_map/gram/pallas_call | solution.py:560
  3.1 4.1 %collective-permute-start = (f32[104,128]{1,0:T(8,128)S(1)}, f32[104,128]{1,0:T(8,128)S(1)}, u32[]{:S(2)}, u32[]{:S(2)}) collective-permute-start(f32[104,128]{1,0:T(8,128)S(1)} %get-tuple-element.18.payload_ref), channel_id=1, source_target_pairs={{0,2},{1,3},{2,0},{3,1},{4,6},{5,7},{6,4},{7,5},{8,10},{9,11},{10,... | collective-permute-start | bytes 159752 | tf_op jit(solution)/shard_map/ppermute | solution.py:550
  7.2 1.4 %collective-permute-start.1 = (f32[32,128]{1,0:T(8,128)S(1)}, f32[32,128]{1,0:T(8,128)S(1)}, u32[]{:S(2)}, u32[]{:S(2)}) collective-permute-start(f32[32,128]{1,0:T(8,128)S(1)} %get-tuple-element.19), channel_id=1, source_target_pairs={{0,30},{1,31},{2,4},{3,5},{4,2},{5,3},{6,8},{7,9},{8,6},{9,7},{10,... | collective-permute-start | bytes 49160 | tf_op jit(solution)/shard_map/ppermute | solution.py:558
  8.6 1.5 %near_own.1 = (f32[1024,128]{1,0:T(8,128)S(1)}, f32[12,8,128]{2,1,0:T(8,128)S(1)}) custom-call(s32[2,11]{1,0:T(2,128)} %list_hbm.1, s32[2]{0:T(128)} %count_hbm.1, f32[104,128]{1,0:T(8,128)S(1)} %get-tuple-element.18.payload_ref, bf16[1024,64]{1,0:T(8,128)(2,1)S(1)} %get-tuple-element.20.target_ref.refs_2_, f32[8,128]{1,0:T(8,128)S(1)} %get-tuple-element.21.centre_ref.refs_1_), custom_call_target="tpu_custom_call" | custom-call | flops 2147483648 | bytes 1048576 | tf_op jit(solution)/shard_map/near_own/pallas_call | solution.py:596
  10.1 2.9 %collective-permute-done.1.side_ref = f32[32,128]{1,0:T(8,128)S(1)} collective-permute-done((f32[32,128]{1,0:T(8,128)S(1)}, f32[32,128]{1,0:T(8,128)S(1)}, u32[]{:S(2)}, u32[]{:S(2)}) %collective-permute-start.1) | collective-permute-done | bytes 16416 | tf_op jit(solution)/shard_map/ppermute | solution.py:558
  13.1 0.0 collective-permute-done.other_ref
  13.1 1.6 %collective-permute-start.2 = (f32[168,128]{1,0:T(8,128)S(1)}, f32[168,128]{1,0:T(8,128)S(1)}, u32[]{:S(2)}, u32[]{:S(2)}) collective-permute-start(f32[168,128]{1,0:T(8,128)S(1)} %merge.1.refs_4_.held_ref), channel_id=1, source_target_pairs={{0,1},{1,0},{2,3},{3,2},{4,5},{5,4},{6,7},{7,6},{8,9},{9,8},{10,11... | collective-permute-start | bytes 258056 | tf_op jit(solution)/shard_map/ppermute | solution.py:550
  14.7 1.3 %near_part.1.before_ref = f32[1024,128]{1,0:T(8,128)S(1)} custom-call(f32[12,8,128]{2,1,0:T(8,128)S(1)} %get-tuple-element.22.refs_0_.flags_ref, f32[8,128]{1,0:T(8,128)S(1)} %get-tuple-element.21.centre_ref.refs_1_, bf16[1024,64]{1,0:T(8,128)(2,1)S(1)} %get-tuple-element.20.target_ref.refs_2_, ...), custom_call_target="tpu_custom_call", output_to_operand_aliasing={{}: (3, {})} | custom-call | flops 2147483648 | bytes 1048576 | tf_op jit(solution)/shard_map/near_part/pallas_call | solution.py:620
  16.0 1.6 %collective-permute-done.2.other_ref = f32[168,128]{1,0:T(8,128)S(1)} collective-permute-done((f32[168,128]{1,0:T(8,128)S(1)}, f32[168,128]{1,0:T(8,128)S(1)}, u32[]{:S(2)}, u32[]{:S(2)}) %collective-permute-start.2) | collective-permute-done | bytes 86048 | tf_op jit(solution)/shard_map/ppermute | solution.py:550
  17.6 5.3 %finish.1 = (f32[8,128]{1,0:T(8,128)}, f32[2,128]{1,0:T(2,128)}, f32[1,32,128]{2,1,0:T(8,128)}, f32[1,32]{1,0:T(1,128)}) custom-call(f32[2,128,128]{2,1,0:T(8,128)S(1)} %get-tuple-element.16.gram_ref, f32[2,128]{1,0:T(2,128)S(1)} %get-tuple-element.17.moment_ref, f32[168,128]{1,0:T(8,128)S(1)} %merge.1.refs_4_.held_ref, ...), custom_call_target="tpu_custom_call" | custom-call | tf_op jit(solution)/shard_map/finish/pallas_call | solution.py:654
  (1 shorter events, 0.0 us)
Async XLA Ops:
  3.1 10.0 %collective-permute-start = (f32[104,128]{1,0:T(8,128)S(1)}, f32[104,128]{1,0:T(8,128)S(1)}, u32[]{:S(2)}, u32[]{:S(2)}) collective-permute-start(f32[104,128]{1,0:T(8,128)S(1)} %get-tuple-element.18.payload_ref), channel_id=1, source_target_pairs={{0,2},{1,3},{2,0},{3,1},{4,6},{5,7},{6,4},{7,5},{8,10},{9,11},{10,... | collective-permute-start | bytes 159752 | tf_op jit(solution)/shard_map/ppermute | solution.py:550
  7.2 5.9 %collective-permute-start.1 = (f32[32,128]{1,0:T(8,128)S(1)}, f32[32,128]{1,0:T(8,128)S(1)}, u32[]{:S(2)}, u32[]{:S(2)}) collective-permute-start(f32[32,128]{1,0:T(8,128)S(1)} %get-tuple-element.19), channel_id=1, source_target_pairs={{0,30},{1,31},{2,4},{3,5},{4,2},{5,3},{6,8},{7,9},{8,6},{9,7},{10,... | collective-permute-start | bytes 49160 | tf_op jit(solution)/shard_map/ppermute | solution.py:558
  13.1 4.6 %collective-permute-start.2 = (f32[168,128]{1,0:T(8,128)S(1)}, f32[168,128]{1,0:T(8,128)S(1)}, u32[]{:S(2)}, u32[]{:S(2)}) collective-permute-start(f32[168,128]{1,0:T(8,128)S(1)} %merge.1.refs_4_.held_ref), channel_id=1, source_target_pairs={{0,1},{1,0},{2,3},{3,2},{4,5},{5,4},{6,7},{7,6},{8,9},{9,8},{10,11... | collective-permute-start | bytes 258056 | tf_op jit(solution)/shard_map/ppermute | solution.py:550

commit v6 on v5

--- a/solution.py
+++ b/solution.py
@@ -553,8 +553,9 @@
         route = []
         for at in range(block_total):
             for z in range(node_count):
-                to = (at + 1 if z >= half else at - 1) % block_total
-                route.append((at * node_count + z, to * node_count + (z ^ half)))
+                to = at + 1 if z >= half else at - 1
+                target = (to, z ^ half) if 0 <= to < block_total else (at, z ^ 1)
+                route.append((at * node_count + z, target[0] * node_count + target[1]))
         return lax.ppermute(block, ("leaf", "node"), route)
 
     points, payload, target, centre, gram, moment = pl.pallas_call(

time: 23.2 us -> 21.7 us (0.935)
  the two profiles are of different devices: /device:TPU:0 before, /device:TPU:4 now
where the time goes in v6:
time: 21.7 us; the launch traced here: 21.4 us
  Pallas kernels  10.5 us (48%)
  waiting for transfers between devices  5.61 us (26%)
  starting transfers between devices  4.68 us (22%)
  between operations  0.66 us (3%)
    pallas_call x1, Pallas kernels, body(): pl.pallas_call(functools.partial(finish_body, node_count=node_count, leaf...  5.26 us
    ppermute x2, starting transfers between devices, across(): lax.ppermute(block, 'node', [(z, z ^ apart) for z in range(node_count)])  4.3 us
    ppermute x1, waiting for transfers between devices, diagonal(): return lax.ppermute(block, ('leaf', 'node'), route)  3.96 us
    pallas_call x1, Pallas kernels, body(): pl.pallas_call(gram_body, out_shape=(jax.ShapeDtypeStruct((points_rows, L...  2.45 us
    ppermute x2, waiting for transfers between devices, across(): lax.ppermute(block, 'node', [(z, z ^ apart) for z in range(node_count)])  1.65 us
    pallas_call x1, Pallas kernels, body(): pl.pallas_call(functools.partial(own_body, node_count=node_count), out_sh...  1.51 us
    pallas_call x1, Pallas kernels, near(): pl.pallas_call(functools.partial(near_body, first=first, last=last, leaf_...  1.26 us
  transfers between devices with their start and end apart: 3, of which 2 were waited for; matrix products, arithmetic and copies ran while one was open for 0% of the time, Pallas kernels for 13%

profile of v6, /device:TPU:4, one launch (start us, length us, event | category | flops | bytes accessed | tf_op | source)
XLA Modules:
  0.0 21.4 jit_solution(3629851048616114579)
XLA Ops:
  0.6 2.5 %gram.1 = (f32[32,128]{1,0:T(8,128)S(1)}, f32[104,128]{1,0:T(8,128)S(1)}, bf16[1024,64]{1,0:T(8,128)(2,1)S(1)}, f32[8,128]{1,0:T(8,128)S(1)}, f32[2,128,128]{2,1,0:T(8,128)S(1)}, /*index=5*/f32[2,128]{1,0:T(2,128)S(1)}) custom-call(f32[3,1024]{1,0:T(4,128)} %positions_hbm.1, f32[8,128]{1,0:T(8,128)} %bitcast.3, f32[1024,128]{1,0:T(8,128)} %far_hbm.1, ...), custom_call_target="tpu_custom_call" | custom-call | tf_op jit(solution)/shard_map/gram/pallas_call | solution.py:561
  3.1 2.7 %collective-permute-start = (f32[104,128]{1,0:T(8,128)S(1)}, f32[104,128]{1,0:T(8,128)S(1)}, u32[]{:S(2)}, u32[]{:S(2)}) collective-permute-start(f32[104,128]{1,0:T(8,128)S(1)} %get-tuple-element.18.payload_ref), channel_id=1, source_target_pairs={{0,2},{1,3},{2,0},{3,1},{4,6},{5,7},{6,4},{7,5},{8,10},{9,11},{10,... | collective-permute-start | bytes 159752 | tf_op jit(solution)/shard_map/ppermute | solution.py:550
  5.7 0.4 %collective-permute-start.1 = (f32[32,128]{1,0:T(8,128)S(1)}, f32[32,128]{1,0:T(8,128)S(1)}, u32[]{:S(2)}, u32[]{:S(2)}) collective-permute-start(f32[32,128]{1,0:T(8,128)S(1)} %get-tuple-element.19), channel_id=1, source_target_pairs={{0,1},{1,0},{2,4},{3,5},{4,2},{5,3},{6,8},{7,9},{8,6},{9,7},{10,12... | collective-permute-start | bytes 49160 | tf_op jit(solution)/shard_map/ppermute | solution.py:559
  6.1 1.5 %near_own.1 = (f32[1024,128]{1,0:T(8,128)S(1)}, f32[12,8,128]{2,1,0:T(8,128)S(1)}) custom-call(s32[2,11]{1,0:T(2,128)} %list_hbm.1, s32[2]{0:T(128)} %count_hbm.1, f32[104,128]{1,0:T(8,128)S(1)} %get-tuple-element.18.payload_ref, bf16[1024,64]{1,0:T(8,128)(2,1)S(1)} %get-tuple-element.20.target_ref.refs_2_, f32[8,128]{1,0:T(8,128)S(1)} %get-tuple-element.21.centre_ref.refs_1_), custom_call_target="tpu_custom_call" | custom-call | flops 2147483648 | bytes 1048576 | tf_op jit(solution)/shard_map/near_own/pallas_call | solution.py:597
  7.7 4.0 %collective-permute-done.1.side_ref = f32[32,128]{1,0:T(8,128)S(1)} collective-permute-done((f32[32,128]{1,0:T(8,128)S(1)}, f32[32,128]{1,0:T(8,128)S(1)}, u32[]{:S(2)}, u32[]{:S(2)}) %collective-permute-start.1) | collective-permute-done | bytes 16416 | tf_op jit(solution)/shard_map/ppermute | solution.py:559
  11.6 0.0 collective-permute-done.other_ref
  11.6 1.6 %collective-permute-start.2 = (f32[168,128]{1,0:T(8,128)S(1)}, f32[168,128]{1,0:T(8,128)S(1)}, u32[]{:S(2)}, u32[]{:S(2)}) collective-permute-start(f32[168,128]{1,0:T(8,128)S(1)} %merge.1.refs_4_.held_ref), channel_id=1, source_target_pairs={{0,1},{1,0},{2,3},{3,2},{4,5},{5,4},{6,7},{7,6},{8,9},{9,8},{10,11... | collective-permute-start | bytes 258056 | tf_op jit(solution)/shard_map/ppermute | solution.py:550
  13.3 1.3 %near_part.1.before_ref = f32[1024,128]{1,0:T(8,128)S(1)} custom-call(f32[12,8,128]{2,1,0:T(8,128)S(1)} %get-tuple-element.22.refs_0_.flags_ref, f32[8,128]{1,0:T(8,128)S(1)} %get-tuple-element.21.centre_ref.refs_1_, bf16[1024,64]{1,0:T(8,128)(2,1)S(1)} %get-tuple-element.20.target_ref.refs_2_, ...), custom_call_target="tpu_custom_call", output_to_operand_aliasing={{}: (3, {})} | custom-call | flops 2147483648 | bytes 1048576 | tf_op jit(solution)/shard_map/near_part/pallas_call | solution.py:621
  14.5 1.6 %collective-permute-done.2.other_ref = f32[168,128]{1,0:T(8,128)S(1)} collective-permute-done((f32[168,128]{1,0:T(8,128)S(1)}, f32[168,128]{1,0:T(8,128)S(1)}, u32[]{:S(2)}, u32[]{:S(2)}) %collective-permute-start.2) | collective-permute-done | bytes 86048 | tf_op jit(solution)/shard_map/ppermute | solution.py:550
  16.2 5.3 %finish.1 = (f32[8,128]{1,0:T(8,128)}, f32[2,128]{1,0:T(2,128)}, f32[1,32,128]{2,1,0:T(8,128)}, f32[1,32]{1,0:T(1,128)}) custom-call(f32[2,128,128]{2,1,0:T(8,128)S(1)} %get-tuple-element.16.gram_ref, f32[2,128]{1,0:T(2,128)S(1)} %get-tuple-element.17.moment_ref, f32[168,128]{1,0:T(8,128)S(1)} %merge.1.refs_4_.held_ref, ...), custom_call_target="tpu_custom_call" | custom-call | tf_op jit(solution)/shard_map/finish/pallas_call | solution.py:655
  (1 shorter events, 0.0 us)
Async XLA Ops:
  3.1 8.5 %collective-permute-start = (f32[104,128]{1,0:T(8,128)S(1)}, f32[104,128]{1,0:T(8,128)S(1)}, u32[]{:S(2)}, u32[]{:S(2)}) collective-permute-start(f32[104,128]{1,0:T(8,128)S(1)} %get-tuple-element.18.payload_ref), channel_id=1, source_target_pairs={{0,2},{1,3},{2,0},{3,1},{4,6},{5,7},{6,4},{7,5},{8,10},{9,11},{10,... | collective-permute-start | bytes 159752 | tf_op jit(solution)/shard_map/ppermute | solution.py:550
  5.7 5.9 %collective-permute-start.1 = (f32[32,128]{1,0:T(8,128)S(1)}, f32[32,128]{1,0:T(8,128)S(1)}, u32[]{:S(2)}, u32[]{:S(2)}) collective-permute-start(f32[32,128]{1,0:T(8,128)S(1)} %get-tuple-element.19), channel_id=1, source_target_pairs={{0,1},{1,0},{2,4},{3,5},{4,2},{5,3},{6,8},{7,9},{8,6},{9,7},{10,12... | collective-permute-start | bytes 49160 | tf_op jit(solution)/shard_map/ppermute | solution.py:559
  11.6 4.6 %collective-permute-start.2 = (f32[168,128]{1,0:T(8,128)S(1)}, f32[168,128]{1,0:T(8,128)S(1)}, u32[]{:S(2)}, u32[]{:S(2)}) collective-permute-start(f32[168,128]{1,0:T(8,128)S(1)} %merge.1.refs_4_.held_ref), channel_id=1, source_target_pairs={{0,1},{1,0},{2,3},{3,2},{4,5},{5,4},{6,7},{7,6},{8,9},{9,8},{10,11... | collective-permute-start | bytes 258056 | tf_op jit(solution)/shard_map/ppermute | solution.py:550

commit v7 on v6

--- a/solution.py
+++ b/solution.py
@@ -95,6 +95,25 @@
     top = jnp.where(lane < half, corner, turned[:half, :])
     bottom = jnp.where((lane < half) | (lane - half >= row), lower, turned[half:, :])
     return jnp.concatenate([top, bottom], axis=0), folded[half + 1 : half + 2, :]
+
+
+def gram_of(response, weights):
+    rank = response.shape[1]
+    parts = [part.astype(jnp.bfloat16) for part in split_parts(response)]
+    right = jnp.concatenate(parts, axis=1)
+    down = (((0,), (0,)), ((), ()))
+    first = lax.dot_general(parts[0], right, down, preferred_element_type=jnp.float32)
+    second = lax.dot_general(parts[1], parts[1], down, preferred_element_type=jnp.float32)
+    mixed = first[:, rank : 2 * rank] + first[:, 2 * rank :]
+    gram = first[:, :rank] + (second + (mixed + jnp.transpose(mixed)))
+    filler = jnp.zeros((2 * SUBLANES - 3, weights.shape[1]), jnp.float32)
+    left = jnp.concatenate([*split_parts(weights), filler], axis=0).astype(jnp.bfloat16)
+    rows = jnp.dot(left, right, preferred_element_type=jnp.float32)
+    moment = rows[0:1, :rank] + (
+        (rows[0:1, rank : 2 * rank] + rows[1:2, :rank])
+        + (rows[0:1, 2 * rank :] + rows[1:2, rank : 2 * rank] + rows[2:3, :rank])
+    )
+    return gram, moment
 
 
 def gram_body(
@@ -146,6 +165,7 @@
     shifted = points - centre
     total_gram = jnp.zeros((rank, rank), jnp.float32)
     total_moment = jnp.zeros((1, rank), jnp.float32)
+    responses = []
     for member in range(per_device):
         span = slice(member * leaf_size, (member + 1) * leaf_size)
         for piece in range(pieces):
@@ -158,20 +178,21 @@
         proxies = jnp.concatenate([proxies_ref[c, member : member + 1, :] for c in range(3)], axis=0)
         source = source_factor(padded_rows(proxies) - centre)
         kernel_values = lax.rsqrt(squares(target, source))
-        copies[4 + member].wait()
-        response = far_ref[span, :] + kernel_values * strengths_ref[member : member + 1, :]
+        responses.append(kernel_values * strengths_ref[member : member + 1, :])
+    for copy in copies[4:]:
+        copy.wait()
+    for member in range(per_device):
+        span = slice(member * leaf_size, (member + 1) * leaf_size)
+        response = far_ref[span, :] + responses[member]
         weights = jnp.concatenate(
             [charges_ref[member * pieces + p : member * pieces + p + 1, :] for p in range(pieces)],
             axis=1,
         )
-        left = jnp.concatenate(
-            [jnp.transpose(response), jnp.broadcast_to(weights, (SUBLANES, leaf_size))], axis=0
-        )
-        both = jnp.dot(left, response, precision=HIGHEST, preferred_element_type=jnp.float32)
-        gram_ref[member] = both[:rank, :]
-        moment_ref[member : member + 1, :] = both[rank : rank + 1, :]
-        total_gram = total_gram + both[:rank, :]
-        total_moment = total_moment + both[rank : rank + 1, :]
+        gram, moment = gram_of(response, weights)
+        gram_ref[member] = gram
+        moment_ref[member : member + 1, :] = moment
+        total_gram = total_gram + gram
+        total_moment = total_moment + moment
     points_rows = per_device * pieces * COORDS
     payload_ref[:points_rows, :] = points_ref[...]
     payload_ref[points_rows:, :] = fold(total_gram, total_moment)

time: 21.7 us -> 21 us (0.968)
  the two profiles are of different devices: /device:TPU:4 before, /device:TPU:12 now
where the time goes in v7:
time: 21 us; the launch traced here: 20.8 us
  Pallas kernels  9.8 us (47%)
  waiting for transfers between devices  6.73 us (32%)
  starting transfers between devices  3.56 us (17%)
  between operations  0.66 us (3%)
    pallas_call x1, Pallas kernels, body(): pl.pallas_call(functools.partial(finish_body, node_count=node_count, leaf...  5.27 us
    ppermute x1, waiting for transfers between devices, diagonal(): return lax.ppermute(block, ('leaf', 'node'), route)  3.96 us
    ppermute x2, starting transfers between devices, across(): lax.ppermute(block, 'node', [(z, z ^ apart) for z in range(node_count)])  3.17 us
    ppermute x2, waiting for transfers between devices, across(): lax.ppermute(block, 'node', [(z, z ^ apart) for z in range(node_count)])  2.77 us
    pallas_call x1, Pallas kernels, body(): pl.pallas_call(gram_body, out_shape=(jax.ShapeDtypeStruct((points_rows, L...  1.76 us
    pallas_call x1, Pallas kernels, body(): pl.pallas_call(functools.partial(own_body, node_count=node_count), out_sh...  1.51 us
    pallas_call x1, Pallas kernels, near(): pl.pallas_call(functools.partial(near_body, first=first, last=last, leaf_...  1.26 us
  transfers between devices with their start and end apart: 3, of which 2 were waited for; matrix products, arithmetic and copies ran while one was open for 0% of the time, Pallas kernels for 13%

profile of v7, /device:TPU:12, one launch (start us, length us, event | category | flops | bytes accessed | tf_op | source)
XLA Modules:
  0.0 20.8 jit_solution(12769286509675126140)
XLA Ops:
  0.6 1.8 %gram.1 = (f32[32,128]{1,0:T(8,128)S(1)}, f32[104,128]{1,0:T(8,128)S(1)}, bf16[1024,64]{1,0:T(8,128)(2,1)S(1)}, f32[8,128]{1,0:T(8,128)S(1)}, f32[2,128,128]{2,1,0:T(8,128)S(1)}, /*index=5*/f32[2,128]{1,0:T(2,128)S(1)}) custom-call(f32[3,1024]{1,0:T(4,128)} %positions_hbm.1, f32[8,128]{1,0:T(8,128)} %bitcast.3, f32[1024,128]{1,0:T(8,128)} %far_hbm.1, ...), custom_call_target="tpu_custom_call" | custom-call | tf_op jit(solution)/shard_map/gram/pallas_call | solution.py:582
  2.4 2.7 %collective-permute-start = (f32[104,128]{1,0:T(8,128)S(1)}, f32[104,128]{1,0:T(8,128)S(1)}, u32[]{:S(2)}, u32[]{:S(2)}) collective-permute-start(f32[104,128]{1,0:T(8,128)S(1)} %get-tuple-element.18.payload_ref), channel_id=1, source_target_pairs={{0,2},{1,3},{2,0},{3,1},{4,6},{5,7},{6,4},{7,5},{8,10},{9,11},{10,... | collective-permute-start | bytes 159752 | tf_op jit(solution)/shard_map/ppermute | solution.py:571
  5.1 0.4 %collective-permute-start.1 = (f32[32,128]{1,0:T(8,128)S(1)}, f32[32,128]{1,0:T(8,128)S(1)}, u32[]{:S(2)}, u32[]{:S(2)}) collective-permute-start(f32[32,128]{1,0:T(8,128)S(1)} %get-tuple-element.19), channel_id=1, source_target_pairs={{0,1},{1,0},{2,4},{3,5},{4,2},{5,3},{6,8},{7,9},{8,6},{9,7},{10,12... | collective-permute-start | bytes 49160 | tf_op jit(solution)/shard_map/ppermute | solution.py:580
  5.4 1.5 %near_own.1 = (f32[1024,128]{1,0:T(8,128)S(1)}, f32[12,8,128]{2,1,0:T(8,128)S(1)}) custom-call(s32[2,11]{1,0:T(2,128)} %list_hbm.1, s32[2]{0:T(128)} %count_hbm.1, f32[104,128]{1,0:T(8,128)S(1)} %get-tuple-element.18.payload_ref, bf16[1024,64]{1,0:T(8,128)(2,1)S(1)} %get-tuple-element.20.target_ref.refs_2_, f32[8,128]{1,0:T(8,128)S(1)} %get-tuple-element.21.centre_ref.refs_1_), custom_call_target="tpu_custom_call" | custom-call | flops 2147483648 | bytes 1048576 | tf_op jit(solution)/shard_map/near_own/pallas_call | solution.py:618
  7.0 4.0 %collective-permute-done.1.side_ref = f32[32,128]{1,0:T(8,128)S(1)} collective-permute-done((f32[32,128]{1,0:T(8,128)S(1)}, f32[32,128]{1,0:T(8,128)S(1)}, u32[]{:S(2)}, u32[]{:S(2)}) %collective-permute-start.1) | collective-permute-done | bytes 16416 | tf_op jit(solution)/shard_map/ppermute | solution.py:580
  10.9 0.0 collective-permute-done.other_ref
  10.9 0.5 %collective-permute-start.2 = (f32[168,128]{1,0:T(8,128)S(1)}, f32[168,128]{1,0:T(8,128)S(1)}, u32[]{:S(2)}, u32[]{:S(2)}) collective-permute-start(f32[168,128]{1,0:T(8,128)S(1)} %merge.1.refs_4_.held_ref), channel_id=1, source_target_pairs={{0,1},{1,0},{2,3},{3,2},{4,5},{5,4},{6,7},{7,6},{8,9},{9,8},{10,11... | collective-permute-start | bytes 258056 | tf_op jit(solution)/shard_map/ppermute | solution.py:571
  11.4 1.3 %near_part.1.before_ref = f32[1024,128]{1,0:T(8,128)S(1)} custom-call(f32[12,8,128]{2,1,0:T(8,128)S(1)} %get-tuple-element.22.refs_0_.flags_ref, f32[8,128]{1,0:T(8,128)S(1)} %get-tuple-element.21.centre_ref.refs_1_, bf16[1024,64]{1,0:T(8,128)(2,1)S(1)} %get-tuple-element.20.target_ref.refs_2_, ...), custom_call_target="tpu_custom_call", output_to_operand_aliasing={{}: (3, {})} | custom-call | flops 2147483648 | bytes 1048576 | tf_op jit(solution)/shard_map/near_part/pallas_call | solution.py:642
  12.7 2.8 %collective-permute-done.2.other_ref = f32[168,128]{1,0:T(8,128)S(1)} collective-permute-done((f32[168,128]{1,0:T(8,128)S(1)}, f32[168,128]{1,0:T(8,128)S(1)}, u32[]{:S(2)}, u32[]{:S(2)}) %collective-permute-start.2) | collective-permute-done | bytes 86048 | tf_op jit(solution)/shard_map/ppermute | solution.py:571
  15.5 5.3 %finish.1 = (f32[8,128]{1,0:T(8,128)}, f32[2,128]{1,0:T(2,128)}, f32[1,32,128]{2,1,0:T(8,128)}, f32[1,32]{1,0:T(1,128)}) custom-call(f32[2,128,128]{2,1,0:T(8,128)S(1)} %get-tuple-element.16.gram_ref, f32[2,128]{1,0:T(2,128)S(1)} %get-tuple-element.17.moment_ref, f32[168,128]{1,0:T(8,128)S(1)} %merge.1.refs_4_.held_ref, ...), custom_call_target="tpu_custom_call" | custom-call | tf_op jit(solution)/shard_map/finish/pallas_call | solution.py:676
  (1 shorter events, 0.0 us)
Async XLA Ops:
  2.4 8.5 %collective-permute-start = (f32[104,128]{1,0:T(8,128)S(1)}, f32[104,128]{1,0:T(8,128)S(1)}, u32[]{:S(2)}, u32[]{:S(2)}) collective-permute-start(f32[104,128]{1,0:T(8,128)S(1)} %get-tuple-element.18.payload_ref), channel_id=1, source_target_pairs={{0,2},{1,3},{2,0},{3,1},{4,6},{5,7},{6,4},{7,5},{8,10},{9,11},{10,... | collective-permute-start | bytes 159752 | tf_op jit(solution)/shard_map/ppermute | solution.py:571
  5.1 5.9 %collective-permute-start.1 = (f32[32,128]{1,0:T(8,128)S(1)}, f32[32,128]{1,0:T(8,128)S(1)}, u32[]{:S(2)}, u32[]{:S(2)}) collective-permute-start(f32[32,128]{1,0:T(8,128)S(1)} %get-tuple-element.19), channel_id=1, source_target_pairs={{0,1},{1,0},{2,4},{3,5},{4,2},{5,3},{6,8},{7,9},{8,6},{9,7},{10,12... | collective-permute-start | bytes 49160 | tf_op jit(solution)/shard_map/ppermute | solution.py:580
  10.9 4.6 %collective-permute-start.2 = (f32[168,128]{1,0:T(8,128)S(1)}, f32[168,128]{1,0:T(8,128)S(1)}, u32[]{:S(2)}, u32[]{:S(2)}) collective-permute-start(f32[168,128]{1,0:T(8,128)S(1)} %merge.1.refs_4_.held_ref), channel_id=1, source_target_pairs={{0,1},{1,0},{2,3},{3,2},{4,5},{5,4},{6,7},{7,6},{8,9},{9,8},{10,11... | collective-permute-start | bytes 258056 | tf_op jit(solution)/shard_map/ppermute | solution.py:571

commit v8 on v7

--- a/solution.py
+++ b/solution.py
@@ -296,71 +296,79 @@
     add_sources(total_ref, None, target_ref, items, flags, per_device, leaf_size)
 
 
-def merge_body(payload_ref, other_ref, side_ref, held_ref, *, rows):
+def points_body(payload_ref, points_ref):
+    points_ref[...] = payload_ref[0 : points_ref.shape[0], :]
+
+
+def merge_body(payload_ref, other_ref, held_ref):
+    rows = payload_ref.shape[0] - fold_rows(payload_ref.shape[1])
     held_ref[0:rows, :] = payload_ref[0:rows, :]
     held_ref[rows : 2 * rows, :] = other_ref[0:rows, :]
-    held_ref[2 * rows : 3 * rows, :] = side_ref[0:rows, :]
-    held_ref[3 * rows :, :] = payload_ref[rows:, :] + other_ref[rows:, :]
-
-
-def near_body(*refs, first, last, leaf_size, source_count):
+    held_ref[2 * rows :, :] = payload_ref[rows:, :] + other_ref[rows:, :]
+
+
+def near_body(*refs, plan, leaf_size, final):
     flags_ref, centre_ref, target_ref, before_ref = refs[:4]
-    source_refs = refs[4 : 4 + source_count]
-    total_ref = refs[4 + source_count]
+    source_refs = refs[4 : 4 + len(plan)]
+    out_ref = refs[4 + len(plan)]
+    total_ref = refs[5 + len(plan)] if final else out_ref
     per_device = target_ref.shape[0] // leaf_size
     leaf_rows = leaf_size // LANES * COORDS
-    group = 3 * per_device
     centre = centre_ref[...]
-
-    def add_group(source_ref, row, number, skip, before_ref):
-        items = [
-            source_blocks(source_ref, row + leaf * leaf_rows, leaf_size, centre)
-            for leaf in range(skip, group)
-        ]
-        flags = [flags_ref[number + leaf] for leaf in range(skip, group)]
-        add_sources(total_ref, before_ref, target_ref, items, flags, per_device, leaf_size)
-
-    number = first // group * group
     before = before_ref
-    for source_ref in source_refs:
-        held = min(last - number, source_ref.shape[0] // leaf_rows) // group
-        add_group(source_ref, 0, number, first % group if before is before_ref else 0, before)
+    for source_ref, (kinds, first, count) in zip(source_refs, plan):
+
+        def add_device(at, before, source_ref=source_ref, kinds=kinds, first=first):
+            items, flags = [], []
+            for place, kind in enumerate(kinds):
+                for member in range(per_device):
+                    if kind is None:
+                        continue
+                    row = ((at * len(kinds) + place) * per_device + member) * leaf_rows
+                    if not isinstance(at, int):
+                        row = pl.multiple_of(row, SUBLANES)
+                    items.append(source_blocks(source_ref, row, leaf_size, centre))
+                    flags.append(flags_ref[((first + at) * 3 + kind) * per_device + member])
+            add_sources(total_ref, before, target_ref, items, flags, per_device, leaf_size)
+
+        add_device(0, before)
         before = total_ref
-        if held > 1:
-
-            def add_more(at, carry, source_ref=source_ref, number=number):
-                row = pl.multiple_of(at * group * leaf_rows, SUBLANES)
-                add_group(source_ref, row, number + at * group, 0, total_ref)
+        if count > 1:
+
+            def add_more(at, carry, add_device=add_device):
+                add_device(at, total_ref)
                 return carry
 
-            lax.fori_loop(1, held, add_more, 0)
-        number += held * group
+            lax.fori_loop(1, count, add_more, 0)
+    if final:
+        for at in range(out_ref.shape[0]):
+            out_ref[at : at + 1, :] = lane_sums(total_ref[at * LANES : (at + 1) * LANES, :])
 
 
 def near_steps(
-    total_ref, out_ref, factor_ref, charge_ref, flags_ref, target_ref, first, leaf_size
+    total_ref, before_ref, factor_ref, charge_ref, flags_ref, target_ref, numbers, leaf_size
 ):
-    count = factor_ref.shape[0]
     per_device = target_ref.shape[0] // leaf_size
     pieces = leaf_size // LANES
 
     def add(at, leaf):
         rows = slice(at * LANES, (at + 1) * LANES)
         member = at // pieces
-        flag = flags_ref[first + leaf][member : member + 1, :]
+        flag = flags_ref[numbers[leaf]][member : member + 1, :]
         weight = charge_ref[leaf][0:1, :] * jnp.concatenate([flag] * pieces, axis=1)
-        term = lax.rsqrt(squares(target_ref[rows, :], factor_ref[leaf])) * weight
-        total_ref[rows, :] += add_tree(
-            [term[:, low : low + LANES] for low in range(0, leaf_size, LANES)]
-        )
-
-    def finish(at):
-        out_ref[at : at + 1, :] = lane_sums(total_ref[at * LANES : (at + 1) * LANES, :])
-
-    steps = []
-    for at in range(per_device * pieces):
-        steps += [functools.partial(add, at, leaf) for leaf in range(count)]
-    return steps + [functools.partial(finish, at) for at in range(per_device * pieces)]
+        total = (before_ref if leaf == 0 else total_ref)[rows, :]
+        for low in range(0, leaf_size, 2 * LANES):
+            lanes = slice(low, low + 2 * LANES)
+            term = lax.rsqrt(squares(target_ref[rows, :], factor_ref[leaf, :, lanes]))
+            term = term * weight[:, lanes]
+            total = total + (term[:, :LANES] + term[:, LANES:])
+        total_ref[rows, :] = total
+
+    return [
+        functools.partial(add, at, leaf)
+        for at in range(per_device * pieces)
+        for leaf in range(len(numbers))
+    ]
 
 
 def add_tree(terms):
@@ -476,17 +484,17 @@
     moment_ref,
     held_ref,
     other_ref,
+    source_ref,
     flags_ref,
     centre_ref,
     target_ref,
     before_ref,
-    near_ref,
+    total_ref,
     coeffs_ref,
     top_factor_ref,
     top_coeffs_ref,
     upper_ref,
     one_ref,
-    total_ref,
     factor_ref,
     charge_ref,
     *,
@@ -510,24 +518,20 @@
         columns = jnp.transpose(jnp.broadcast_to(moment, (rank, rank)))
         moments.append([columns[SUBLANES * i : SUBLANES * (i + 1), :] for i in range(block_count)])
 
-    group = factor_ref.shape[0]
     leaf_rows = leaf_size // LANES * COORDS
-    points_rows = other_ref.shape[0] - fold_rows(rank)
     centre = centre_ref[...]
-    for leaf in range(group):
-        row = points_rows - (group - leaf) * leaf_rows
-        factor, charge = source_blocks(other_ref, row, leaf_size, centre)
+    for leaf in range(factor_ref.shape[0]):
+        factor, charge = source_blocks(source_ref, leaf * leaf_rows, leaf_size, centre)
         factor_ref[leaf] = factor
         charge_ref[leaf, 0:1, :] = charge
-    total_ref[...] = before_ref[...]
     steps = near_steps(
         total_ref,
-        near_ref,
+        before_ref,
         factor_ref,
         charge_ref,
         flags_ref,
         target_ref,
-        flags_ref.shape[0] - group,
+        [3 * per_device + leaf for leaf in range(factor_ref.shape[0])],
         leaf_size,
     )
 
@@ -614,6 +618,14 @@
     params = pltpu.CompilerParams(vmem_limit_bytes=VMEM_LIMIT)
     work = pl.CostEstimate(flops=1 << 31, bytes_accessed=1 << 20, transcendentals=0)
     other_half = across(payload, half)
+    points = pl.pallas_call(
+        points_body,
+        out_shape=jax.ShapeDtypeStruct(points.shape, f32),
+        in_specs=[VMEM_SPEC],
+        out_specs=VMEM_SPEC,
+        compiler_params=params,
+        name="points",
+    )(payload)
     side = diagonal(points)
     total, flags = pl.pallas_call(
         functools.partial(own_body, node_count=node_count),
@@ -630,69 +642,71 @@
         name="near_own",
     )(in_hbm(near_list), in_hbm(near_count), payload, target, centre)
     held = pl.pallas_call(
-        functools.partial(merge_body, rows=points_rows),
-        out_shape=jax.ShapeDtypeStruct((3 * points_rows + fold_rows(rank), rank), f32),
-        in_specs=[VMEM_SPEC] * 3,
+        merge_body,
+        out_shape=jax.ShapeDtypeStruct((2 * points_rows + fold_rows(rank), rank), f32),
+        in_specs=[VMEM_SPEC] * 2,
         out_specs=VMEM_SPEC,
         compiler_params=params,
         name="merge",
-    )(payload, other_half, side)
-
-    def near(first, last, sources):
+    )(payload, other_half)
+
+    def near(plan, sources, total, final):
         return pl.pallas_call(
-            functools.partial(
-                near_body,
-                first=first,
-                last=last,
-                leaf_size=leaf_size,
-                source_count=len(sources),
-            ),
-            out_shape=totals,
+            functools.partial(near_body, plan=plan, leaf_size=leaf_size, final=final),
+            out_shape=jax.ShapeDtypeStruct((per_device * pieces, LANES), f32) if final else totals,
             in_specs=[VMEM_SPEC] * (4 + len(sources)),
             out_specs=VMEM_SPEC,
-            input_output_aliases={3: 0},
+            scratch_shapes=[pltpu.VMEM(totals.shape, f32)] if final else [],
+            input_output_aliases={} if final else {3: 0},
             compiler_params=params,
             cost_estimate=work,
-            name="near_part",
+            name="near_last" if final else "near_part",
         )(flags, centre, target, total, *sources)
 
-    group = 3 * per_device
+    last_plan, last_sources = [], []
     arrived = []
     apart = 1
     while apart < half:
         arrived.append(across(held, apart))
         if apart == 1:
-            total = near(per_device, group, [held])
+            total = near([((None, 1), 0, 1)], [held], total, False)
+            side, total = lax.optimization_barrier((side, total))
+            total = near([((2,), 0, 1)], [side], total, False)
+        else:
+            last_plan.append(((0, 1), apart, apart))
+            last_sources.append(arrived[-1])
+        last_plan.append(((2,), apart, apart))
+        last_sources.append(across(side, apart))
         if 2 * apart < half:
             rows = held.shape[0] - fold_rows(rank)
             held = jnp.concatenate(
                 [held[:rows], arrived[-1][:rows], held[rows:] + arrived[-1][rows:]]
             )
+            side = jnp.concatenate([side, last_sources[-1]])
         apart *= 2
-    if numbers > 2 * group:
-        total = near(group, numbers - group, arrived)
 
     share = rank // node_count
-    potential, coeffs, top_factor, top_coeffs = pl.pallas_call(
+    total, coeffs, top_factor, top_coeffs = pl.pallas_call(
         functools.partial(finish_body, node_count=node_count, leaf_size=leaf_size),
         out_shape=(
-            jax.ShapeDtypeStruct((per_device * pieces, LANES), f32),
+            totals,
             jax.ShapeDtypeStruct((per_device, rank), f32),
             jax.ShapeDtypeStruct((1, share, rank), f32),
             jax.ShapeDtypeStruct((1, share), f32),
         ),
-        in_specs=[VMEM_SPEC] * 8,
+        in_specs=[VMEM_SPEC] * 9,
         out_specs=(VMEM_SPEC,) * 4,
         scratch_shapes=[
             pltpu.VMEM((per_device + 1, rank, rank), f32),
             pltpu.VMEM((SUBLANES, rank), f32),
-            pltpu.VMEM(totals.shape, f32),
-            pltpu.VMEM((group, SUBLANES * len(PART_PAIRS), leaf_size), jnp.bfloat16),
-            pltpu.VMEM((group, SUBLANES, leaf_size), f32),
+            pltpu.VMEM((2 * per_device, SUBLANES * len(PART_PAIRS), leaf_size), jnp.bfloat16),
+            pltpu.VMEM((2 * per_device, SUBLANES, leaf_size), f32),
         ],
         compiler_params=params,
+        cost_estimate=work,
         name="finish",
-    )(gram, moment, held, arrived[-1], flags, centre, target, total)
+    )(gram, moment, held, arrived[-1], arrived[0], flags, centre, target, total)
+    potential = near(last_plan, last_sources, total, True)
     return (potential.reshape(-1), coeffs, top_factor, top_coeffs)
 
 

time: 21 us -> 20.9 us (level)
  the two profiles are of different devices: /device:TPU:12 before, /device:TPU:0 now
where the time goes in v8:
time: 20.9 us; the launch traced here: 20.6 us
  Pallas kernels  11.2 us (54%)
  starting transfers between devices  7.83 us (37%)
  waiting for transfers between devices  0.95 us (5%)
  between operations  0.69 us (3%)
    ppermute x3, starting transfers between devices, across(): lax.ppermute(block, 'node', [(z, z ^ apart) for z in range(node_count)])  6.26 us
    pallas_call x1, Pallas kernels, body(): pl.pallas_call(functools.partial(finish_body, node_count=node_count, leaf...  4.9 us
    pallas_call x3, Pallas kernels, near(): pl.pallas_call(functools.partial(near_body, plan=plan, leaf_size=leaf_siz...  2.97 us
    pallas_call x1, Pallas kernels, body(): pl.pallas_call(gram_body, out_shape=(jax.ShapeDtypeStruct((points_rows, L...  1.77 us
    ppermute x1, starting transfers between devices, diagonal(): return lax.ppermute(block, ('leaf', 'node'), route)  1.58 us
    pallas_call x1, Pallas kernels, body(): pl.pallas_call(functools.partial(own_body, node_count=node_count), out_sh...  1.51 us
    ppermute x3, waiting for transfers between devices, across(): lax.ppermute(block, 'node', [(z, z ^ apart) for z in range(node_count)])  0.95 us
  transfers between devices with their start and end apart: 4, of which 1 were waited for; matrix products, arithmetic and copies ran while one was open for 0% of the time, Pallas kernels for 38%

profile of v8, /device:TPU:0, one launch (start us, length us, event | category | flops | bytes accessed | tf_op | source)
XLA Modules:
  0.0 20.6 jit_solution(7761807217116113907)
XLA Ops:
  0.6 1.8 %gram.1 = (f32[32,128]{1,0:T(8,128)}, f32[104,128]{1,0:T(8,128)S(1)}, bf16[1024,64]{1,0:T(8,128)(2,1)S(1)}, f32[8,128]{1,0:T(8,128)S(1)}, f32[2,128,128]{2,1,0:T(8,128)S(1)}, /*index=5*/f32[2,128]{1,0:T(2,128)S(1)}) custom-call(f32[3,1024]{1,0:T(4,128)} %positions_hbm.1, f32[8,128]{1,0:T(8,128)} %bitcast.3, f32[1024,128]{1,0:T(8,128)} %far_hbm.1, ...), custom_call_target="tpu_custom_call" | custom-call | tf_op jit(solution)/shard_map/gram/pallas_call | solution.py:586
  2.4 4.1 %collective-permute-start = (f32[104,128]{1,0:T(8,128)S(1)}, f32[104,128]{1,0:T(8,128)S(1)}, u32[]{:S(2)}, u32[]{:S(2)}) collective-permute-start(f32[104,128]{1,0:T(8,128)S(1)} %get-tuple-element.17.payload_ref), channel_id=1, source_target_pairs={{0,2},{1,3},{2,0},{3,1},{4,6},{5,7},{6,4},{7,5},{8,10},{9,11},{10,... | collective-permute-start | bytes 159752 | tf_op jit(solution)/shard_map/ppermute | solution.py:575
  6.5 1.6 %collective-permute-start.2 = (f32[32,128]{1,0:T(8,128)S(1)}, f32[32,128]{1,0:T(8,128)S(1)}, u32[]{:S(2)}, u32[]{:S(2)}) collective-permute-start(f32[32,128]{1,0:T(8,128)S(1)} %points.1), channel_id=1, source_target_pairs={{0,1},{1,0},{2,4},{3,5},{4,2},{5,3},{6,8},{7,9},{8,6},{9,7},{10,12... | collective-permute-start | bytes 49160 | tf_op jit(solution)/shard_map/ppermute | solution.py:584
  8.1 1.5 %near_own.1 = (f32[1024,128]{1,0:T(8,128)S(1)}, f32[12,8,128]{2,1,0:T(8,128)S(1)}) custom-call(s32[2,11]{1,0:T(2,128)} %list_hbm.1, s32[2]{0:T(128)} %count_hbm.1, f32[104,128]{1,0:T(8,128)S(1)} %get-tuple-element.17.payload_ref, bf16[1024,64]{1,0:T(8,128)(2,1)S(1)} %get-tuple-element.18.target_ref.refs_2_, f32[8,128]{1,0:T(8,128)S(1)} %get-tuple-element.19.centre_ref.refs_1_), custom_call_target="tpu_custom_call" | custom-call | flops 2147483648 | bytes 1048576 | tf_op jit(solution)/shard_map/near_own/pallas_call | solution.py:630
  9.6 0.0 collective-permute-done.other_ref
  9.6 1.0 %collective-permute-start.1 = (f32[136,128]{1,0:T(8,128)S(1)}, f32[136,128]{1,0:T(8,128)S(1)}, u32[]{:S(2)}, u32[]{:S(2)}) collective-permute-start(f32[136,128]{1,0:T(8,128)S(1)} %merge.1.refs_4_.held_ref), channel_id=1, source_target_pairs={{0,1},{1,0},{2,3},{3,2},{4,5},{5,4},{6,7},{7,6},{8,9},{9,8},{10,11... | collective-permute-start | bytes 208904 | tf_op jit(solution)/shard_map/ppermute | solution.py:575
  10.6 0.7 %near_part.2.refs_3_ = f32[1024,128]{1,0:T(8,128)S(1)} custom-call(f32[12,8,128]{2,1,0:T(8,128)S(1)} %get-tuple-element.20.refs_0_.flags_ref, f32[8,128]{1,0:T(8,128)S(1)} %get-tuple-element.19.centre_ref.refs_1_, bf16[1024,64]{1,0:T(8,128)(2,1)S(1)} %get-tuple-element.18.target_ref.refs_2_, ...), custom_call_target="tpu_custom_call", output_to_operand_aliasing={{}: (3, {})} | custom-call | flops 2147483648 | bytes 1048576 | tf_op jit(solution)/shard_map/near_part/pallas_call | solution.py:654
  11.3 0.0 collective-permute-done.2.refs_4_
  11.4 1.2 %collective-permute-start.3 = (f32[32,128]{1,0:T(8,128)S(1)}, f32[32,128]{1,0:T(8,128)S(1)}, u32[]{:S(2)}, u32[]{:S(2)}) collective-permute-start(f32[32,128]{1,0:T(8,128)S(1)} %collective-permute-done.2.refs_4_), channel_id=1, source_target_pairs={{0,1},{1,0},{2,3},{3,2},{4,5},{5,4},{6,7},{7,6},{8,9},{9,8},{10,11... | collective-permute-start | bytes 49160 | tf_op jit(solution)/shard_map/ppermute | solution.py:575
  12.5 0.7 %near_part.3.before_ref = f32[1024,128]{1,0:T(8,128)S(1)} custom-call(f32[12,8,128]{2,1,0:T(8,128)S(1)} %get-tuple-element.20.refs_0_.flags_ref, f32[8,128]{1,0:T(8,128)S(1)} %get-tuple-element.19.centre_ref.refs_1_, bf16[1024,64]{1,0:T(8,128)(2,1)S(1)} %get-tuple-element.18.target_ref.refs_2_, ...), custom_call_target="tpu_custom_call", output_to_operand_aliasing={{}: (3, {})} | custom-call | flops 2147483648 | bytes 1048576 | tf_op jit(solution)/shard_map/near_part/pallas_call | solution.py:654
  13.2 0.9 %collective-permute-done.1.other_ref.source_ref = f32[136,128]{1,0:T(8,128)S(1)} collective-permute-done((f32[136,128]{1,0:T(8,128)S(1)}, f32[136,128]{1,0:T(8,128)S(1)}, u32[]{:S(2)}, u32[]{:S(2)}) %collective-permute-start.1) | collective-permute-done | bytes 69664 | tf_op jit(solution)/shard_map/ppermute | solution.py:575
  14.2 4.9 %finish.1 = (f32[1024,128]{1,0:T(8,128)S(1)}, f32[2,128]{1,0:T(2,128)}, f32[1,32,128]{2,1,0:T(8,128)}, f32[1,32]{1,0:T(1,128)}) custom-call(f32[2,128,128]{2,1,0:T(8,128)S(1)} %get-tuple-element.21.gram_ref, f32[2,128]{1,0:T(2,128)S(1)} %get-tuple-element.22.moment_ref, f32[136,128]{1,0:T(8,128)S(1)} %merge.1.refs_4_.held_ref, ...), custom_call_target="tpu_custom_call" | custom-call | flops 2147483648 | bytes 1048576 | tf_op jit(solution)/shard_map/finish/pallas_call | solution.py:689
  19.1 0.0 collective-permute-done.3.refs_4_
  19.1 1.5 %near_last.1 = f32[8,128]{1,0:T(8,128)} custom-call(f32[12,8,128]{2,1,0:T(8,128)S(1)} %get-tuple-element.20.refs_0_.flags_ref, f32[8,128]{1,0:T(8,128)S(1)} %get-tuple-element.19.centre_ref.refs_1_, bf16[1024,64]{1,0:T(8,128)(2,1)S(1)} %get-tuple-element.18.target_ref.refs_2_, f32[1024,128]{1,0:T(8,128)S(1)} %get-tuple-element.26.refs_3_, ...), custom_call_target="tpu_custom_call" | custom-call | flops 2147483648 | bytes 1048576 | tf_op jit(solution)/shard_map/near_last/pallas_call | solution.py:654
  (2 shorter events, 0.0 us)
Async XLA Ops:
  2.4 7.2 %collective-permute-start = (f32[104,128]{1,0:T(8,128)S(1)}, f32[104,128]{1,0:T(8,128)S(1)}, u32[]{:S(2)}, u32[]{:S(2)}) collective-permute-start(f32[104,128]{1,0:T(8,128)S(1)} %get-tuple-element.17.payload_ref), channel_id=1, source_target_pairs={{0,2},{1,3},{2,0},{3,1},{4,6},{5,7},{6,4},{7,5},{8,10},{9,11},{10,... | collective-permute-start | bytes 159752 | tf_op jit(solution)/shard_map/ppermute | solution.py:575
  6.5 4.8 %collective-permute-start.2 = (f32[32,128]{1,0:T(8,128)S(1)}, f32[32,128]{1,0:T(8,128)S(1)}, u32[]{:S(2)}, u32[]{:S(2)}) collective-permute-start(f32[32,128]{1,0:T(8,128)S(1)} %points.1), channel_id=1, source_target_pairs={{0,1},{1,0},{2,4},{3,5},{4,2},{5,3},{6,8},{7,9},{8,6},{9,7},{10,12... | collective-permute-start | bytes 49160 | tf_op jit(solution)/shard_map/ppermute | solution.py:584
  9.6 4.5 %collective-permute-start.1 = (f32[136,128]{1,0:T(8,128)S(1)}, f32[136,128]{1,0:T(8,128)S(1)}, u32[]{:S(2)}, u32[]{:S(2)}) collective-permute-start(f32[136,128]{1,0:T(8,128)S(1)} %merge.1.refs_4_.held_ref), channel_id=1, source_target_pairs={{0,1},{1,0},{2,3},{3,2},{4,5},{5,4},{6,7},{7,6},{8,9},{9,8},{10,11... | collective-permute-start | bytes 208904 | tf_op jit(solution)/shard_map/ppermute | solution.py:575
  11.4 7.7 %collective-permute-start.3 = (f32[32,128]{1,0:T(8,128)S(1)}, f32[32,128]{1,0:T(8,128)S(1)}, u32[]{:S(2)}, u32[]{:S(2)}) collective-permute-start(f32[32,128]{1,0:T(8,128)S(1)} %collective-permute-done.2.refs_4_), channel_id=1, source_target_pairs={{0,1},{1,0},{2,3},{3,2},{4,5},{5,4},{6,7},{7,6},{8,9},{9,8},{10,11... | collective-permute-start | bytes 49160 | tf_op jit(solution)/shard_map/ppermute | solution.py:575

commit v9 on v8

--- a/solution.py
+++ b/solution.py
@@ -15,7 +15,7 @@
 LANES = 128
 COORDS = 4
 VMEM_LIMIT = 16 << 20
-PART_PAIRS = ((0, 0), (0, 1), (1, 0), (1, 1), (0, 2), (2, 0), (1, 2), (2, 1))
+PART_PAIRS = ((0, 0), (0, 1), (1, 0), (1, 1), (0, 2), (2, 0))
 
 
 def split_parts(block):

time: 20.9 us -> 21.1 us (level)
  transfers between devices with their start and end apart: 4 -> 4, of which waited for: 1 -> 1; matrix products, arithmetic and copies ran while one was open for 0% -> 0% of each run, Pallas kernels for 38% -> 39%
where the time goes in v9:
time: 21.1 us; the launch traced here: 20.8 us
  Pallas kernels  11.4 us (54%)
  starting transfers between devices  7.83 us (37%)
  waiting for transfers between devices  0.94 us (4%)
  between operations  0.69 us (3%)
    ppermute x3, starting transfers between devices, across(): lax.ppermute(block, 'node', [(z, z ^ apart) for z in range(node_count)])  6.25 us
    pallas_call x1, Pallas kernels, body(): pl.pallas_call(functools.partial(finish_body, node_count=node_count, leaf...  5.11 us
    pallas_call x3, Pallas kernels, near(): pl.pallas_call(functools.partial(near_body, plan=plan, leaf_size=leaf_siz...  2.96 us
    pallas_call x1, Pallas kernels, body(): pl.pallas_call(gram_body, out_shape=(jax.ShapeDtypeStruct((points_rows, L...  1.77 us
    ppermute x1, starting transfers between devices, diagonal(): return lax.ppermute(block, ('leaf', 'node'), route)  1.58 us
    pallas_call x1, Pallas kernels, body(): pl.pallas_call(functools.partial(own_body, node_count=node_count), out_sh...  1.5 us
    ppermute x3, waiting for transfers between devices, across(): lax.ppermute(block, 'node', [(z, z ^ apart) for z in range(node_count)])  0.94 us
  transfers between devices with their start and end apart: 4, of which 1 were waited for; matrix products, arithmetic and copies ran while one was open for 0% of the time, Pallas kernels for 39%

profile of v9, /device:TPU:0, one launch (start us, length us, event | category | flops | bytes accessed | tf_op | source)
XLA Modules:
  0.0 20.8 jit_solution(1693338906689268178)
XLA Ops:
  0.6 1.8 %gram.1 = (f32[32,128]{1,0:T(8,128)}, f32[104,128]{1,0:T(8,128)S(1)}, bf16[1024,48]{1,0:T(8,128)(2,1)S(1)}, f32[8,128]{1,0:T(8,128)S(1)}, f32[2,128,128]{2,1,0:T(8,128)S(1)}, /*index=5*/f32[2,128]{1,0:T(2,128)S(1)}) custom-call(f32[3,1024]{1,0:T(4,128)} %positions_hbm.1, f32[8,128]{1,0:T(8,128)} %bitcast.3, f32[1024,128]{1,0:T(8,128)} %far_hbm.1, ...), custom_call_target="tpu_custom_call" | custom-call | tf_op jit(solution)/shard_map/gram/pallas_call | solution.py:586
  2.4 4.1 %collective-permute-start = (f32[104,128]{1,0:T(8,128)S(1)}, f32[104,128]{1,0:T(8,128)S(1)}, u32[]{:S(2)}, u32[]{:S(2)}) collective-permute-start(f32[104,128]{1,0:T(8,128)S(1)} %get-tuple-element.17.payload_ref), channel_id=1, source_target_pairs={{0,2},{1,3},{2,0},{3,1},{4,6},{5,7},{6,4},{7,5},{8,10},{9,11},{10,... | collective-permute-start | bytes 159752 | tf_op jit(solution)/shard_map/ppermute | solution.py:575
  6.5 1.6 %collective-permute-start.2 = (f32[32,128]{1,0:T(8,128)S(1)}, f32[32,128]{1,0:T(8,128)S(1)}, u32[]{:S(2)}, u32[]{:S(2)}) collective-permute-start(f32[32,128]{1,0:T(8,128)S(1)} %points.1), channel_id=1, source_target_pairs={{0,1},{1,0},{2,4},{3,5},{4,2},{5,3},{6,8},{7,9},{8,6},{9,7},{10,12... | collective-permute-start | bytes 49160 | tf_op jit(solution)/shard_map/ppermute | solution.py:584
  8.1 1.5 %near_own.1 = (f32[1024,128]{1,0:T(8,128)S(1)}, f32[12,8,128]{2,1,0:T(8,128)S(1)}) custom-call(s32[2,11]{1,0:T(2,128)} %list_hbm.1, s32[2]{0:T(128)} %count_hbm.1, f32[104,128]{1,0:T(8,128)S(1)} %get-tuple-element.17.payload_ref, bf16[1024,48]{1,0:T(8,128)(2,1)S(1)} %get-tuple-element.18.target_ref.refs_2_, f32[8,128]{1,0:T(8,128)S(1)} %get-tuple-element.19.centre_ref.refs_1_), custom_call_target="tpu_custom_call" | custom-call | flops 2147483648 | bytes 1048576 | tf_op jit(solution)/shard_map/near_own/pallas_call | solution.py:630
  9.6 0.0 collective-permute-done.other_ref
  9.6 1.0 %collective-permute-start.1 = (f32[136,128]{1,0:T(8,128)S(1)}, f32[136,128]{1,0:T(8,128)S(1)}, u32[]{:S(2)}, u32[]{:S(2)}) collective-permute-start(f32[136,128]{1,0:T(8,128)S(1)} %merge.1.refs_4_.held_ref), channel_id=1, source_target_pairs={{0,1},{1,0},{2,3},{3,2},{4,5},{5,4},{6,7},{7,6},{8,9},{9,8},{10,11... | collective-permute-start | bytes 208904 | tf_op jit(solution)/shard_map/ppermute | solution.py:575
  10.6 0.7 %near_part.2.refs_3_ = f32[1024,128]{1,0:T(8,128)S(1)} custom-call(f32[12,8,128]{2,1,0:T(8,128)S(1)} %get-tuple-element.20.refs_0_.flags_ref, f32[8,128]{1,0:T(8,128)S(1)} %get-tuple-element.19.centre_ref.refs_1_, bf16[1024,48]{1,0:T(8,128)(2,1)S(1)} %get-tuple-element.18.target_ref.refs_2_, ...), custom_call_target="tpu_custom_call", output_to_operand_aliasing={{}: (3, {})} | custom-call | flops 2147483648 | bytes 1048576 | tf_op jit(solution)/shard_map/near_part/pallas_call | solution.py:654
  11.3 0.0 collective-permute-done.2.refs_4_
  11.4 1.2 %collective-permute-start.3 = (f32[32,128]{1,0:T(8,128)S(1)}, f32[32,128]{1,0:T(8,128)S(1)}, u32[]{:S(2)}, u32[]{:S(2)}) collective-permute-start(f32[32,128]{1,0:T(8,128)S(1)} %collective-permute-done.2.refs_4_), channel_id=1, source_target_pairs={{0,1},{1,0},{2,3},{3,2},{4,5},{5,4},{6,7},{7,6},{8,9},{9,8},{10,11... | collective-permute-start | bytes 49160 | tf_op jit(solution)/shard_map/ppermute | solution.py:575
  12.5 0.7 %near_part.3.before_ref = f32[1024,128]{1,0:T(8,128)S(1)} custom-call(f32[12,8,128]{2,1,0:T(8,128)S(1)} %get-tuple-element.20.refs_0_.flags_ref, f32[8,128]{1,0:T(8,128)S(1)} %get-tuple-element.19.centre_ref.refs_1_, bf16[1024,48]{1,0:T(8,128)(2,1)S(1)} %get-tuple-element.18.target_ref.refs_2_, ...), custom_call_target="tpu_custom_call", output_to_operand_aliasing={{}: (3, {})} | custom-call | flops 2147483648 | bytes 1048576 | tf_op jit(solution)/shard_map/near_part/pallas_call | solution.py:654
  13.2 0.9 %collective-permute-done.1.other_ref.source_ref = f32[136,128]{1,0:T(8,128)S(1)} collective-permute-done((f32[136,128]{1,0:T(8,128)S(1)}, f32[136,128]{1,0:T(8,128)S(1)}, u32[]{:S(2)}, u32[]{:S(2)}) %collective-permute-start.1) | collective-permute-done | bytes 69664 | tf_op jit(solution)/shard_map/ppermute | solution.py:575
  14.2 5.1 %finish.1 = (f32[1024,128]{1,0:T(8,128)S(1)}, f32[2,128]{1,0:T(2,128)}, f32[1,32,128]{2,1,0:T(8,128)}, f32[1,32]{1,0:T(1,128)}) custom-call(f32[2,128,128]{2,1,0:T(8,128)S(1)} %get-tuple-element.21.gram_ref, f32[2,128]{1,0:T(2,128)S(1)} %get-tuple-element.22.moment_ref, f32[136,128]{1,0:T(8,128)S(1)} %merge.1.refs_4_.held_ref, ...), custom_call_target="tpu_custom_call" | custom-call | flops 2147483648 | bytes 1048576 | tf_op jit(solution)/shard_map/finish/pallas_call | solution.py:689
  19.3 0.0 collective-permute-done.3.refs_4_
  19.3 1.5 %near_last.1 = f32[8,128]{1,0:T(8,128)} custom-call(f32[12,8,128]{2,1,0:T(8,128)S(1)} %get-tuple-element.20.refs_0_.flags_ref, f32[8,128]{1,0:T(8,128)S(1)} %get-tuple-element.19.centre_ref.refs_1_, bf16[1024,48]{1,0:T(8,128)(2,1)S(1)} %get-tuple-element.18.target_ref.refs_2_, f32[1024,128]{1,0:T(8,128)S(1)} %get-tuple-element.26.refs_3_, ...), custom_call_target="tpu_custom_call" | custom-call | flops 2147483648 | bytes 1048576 | tf_op jit(solution)/shard_map/near_last/pallas_call | solution.py:654
  (2 shorter events, 0.0 us)
Async XLA Ops:
  2.4 7.2 %collective-permute-start = (f32[104,128]{1,0:T(8,128)S(1)}, f32[104,128]{1,0:T(8,128)S(1)}, u32[]{:S(2)}, u32[]{:S(2)}) collective-permute-start(f32[104,128]{1,0:T(8,128)S(1)} %get-tuple-element.17.payload_ref), channel_id=1, source_target_pairs={{0,2},{1,3},{2,0},{3,1},{4,6},{5,7},{6,4},{7,5},{8,10},{9,11},{10,... | collective-permute-start | bytes 159752 | tf_op jit(solution)/shard_map/ppermute | solution.py:575
  6.5 4.8 %collective-permute-start.2 = (f32[32,128]{1,0:T(8,128)S(1)}, f32[32,128]{1,0:T(8,128)S(1)}, u32[]{:S(2)}, u32[]{:S(2)}) collective-permute-start(f32[32,128]{1,0:T(8,128)S(1)} %points.1), channel_id=1, source_target_pairs={{0,1},{1,0},{2,4},{3,5},{4,2},{5,3},{6,8},{7,9},{8,6},{9,7},{10,12... | collective-permute-start | bytes 49160 | tf_op jit(solution)/shard_map/ppermute | solution.py:584
  9.6 4.5 %collective-permute-start.1 = (f32[136,128]{1,0:T(8,128)S(1)}, f32[136,128]{1,0:T(8,128)S(1)}, u32[]{:S(2)}, u32[]{:S(2)}) collective-permute-start(f32[136,128]{1,0:T(8,128)S(1)} %merge.1.refs_4_.held_ref), channel_id=1, source_target_pairs={{0,1},{1,0},{2,3},{3,2},{4,5},{5,4},{6,7},{7,6},{8,9},{9,8},{10,11... | collective-permute-start | bytes 208904 | tf_op jit(solution)/shard_map/ppermute | solution.py:575
  11.4 7.9 %collective-permute-start.3 = (f32[32,128]{1,0:T(8,128)S(1)}, f32[32,128]{1,0:T(8,128)S(1)}, u32[]{:S(2)}, u32[]{:S(2)}) collective-permute-start(f32[32,128]{1,0:T(8,128)S(1)} %collective-permute-done.2.refs_4_), channel_id=1, source_target_pairs={{0,1},{1,0},{2,3},{3,2},{4,5},{5,4},{6,7},{7,6},{8,9},{9,8},{10,11... | collective-permute-start | bytes 49160 | tf_op jit(solution)/shard_map/ppermute | solution.py:575
